TPU v7x, 512 devices: a whole 4x4x16 slice. The times are simulated.
512 devices in a mesh: fx: 8 (over z_lo, core), fy: 16 (over y, x), dp: 4 (over z_hi).
Axes of the slice: x: 4, y: 4, z: 16 (z_hi: 4, z_lo: 4; z = z_hi * 4 + z_lo), core: 2. Of those that a mesh axis runs over, the one named last changes fastest.
Arguments:
- hidden_in: bfloat16 [4, 128, 128, 1152], P('dp', ('fx', 'fy')), may hold values from -6 to 6
- spatial_triple: bfloat16 [4, 128, 128, 1728], P('dp', ('fx', 'fy')), may hold values from -6 to 6
- context_grad: bfloat16 [4, 128, 128, 576], P('dp', None, ('fx', 'fy')), may hold values from -6 to 6
- out_weight: bfloat16 [576, 1152], P(None, ('fx', 'fy')), may hold values from -0.25 to 0.25
- triple_weight: bfloat16 [1152, 1728], P(('fx', 'fy')), may hold values from -0.1875 to 0.1875
Outputs:
- grad_triple: bfloat16 [4, 128, 128, 1728], P('dp', ('fx', 'fy'))
- grad_hidden: bfloat16 [4, 128, 128, 1152], P('dp', ('fx', 'fy'))
- grad_out_weight: float32 [576, 1152], P(None, ('fx', 'fy'))
All inputs are finite; a program needn't handle non-finite values.
Results may differ from a plain program's by a relative error of at most 0.03.
Values may be sent and summed in bfloat16 or wider, within the bound.
No kernel may reach another device: no remote copies, remote signals or barrier semaphores. Data moves between devices by JAX's collectives and lax.ppermute only.
A program may use at most 64 MiB of HBM per device.

v0:
```python
from functools import partial
import math

import jax
import jax.numpy as jnp
from jax import lax
from jax.sharding import PartitionSpec as P

HEADS = 8


def attention(triple, heads):
    batch, length, total_width = triple.shape
    size_head = total_width // (3 * heads)
    parts = triple.reshape(batch, length, 3, heads, size_head)
    query = parts[:, :, 0]
    keys = parts[:, :, 1]
    values = parts[:, :, 2]
    scores = jnp.einsum(
        "bqhe,bkhe->bhqk", query, keys, precision=lax.Precision.HIGHEST
    ) / math.sqrt(size_head)
    weights = jnp.exp(scores)
    weights = weights / jnp.sum(weights, axis=-1, keepdims=True)
    output = jnp.einsum("bhqk,bkhe->bqhe", weights, values, precision=lax.Precision.HIGHEST)
    return output.reshape(batch, length, heads * size_head)


def normalize(hidden):
    centre = jnp.mean(hidden, axis=-1, keepdims=True)
    centred = hidden - centre
    spread = jnp.mean(centred * centred, axis=-1, keepdims=True)
    return centred * lax.rsqrt(spread + 1e-06)


def to_columns(block):
    clips, frames, patches, width = block.shape
    group = lax.axis_size(("fx", "fy"))
    columns = patches // group
    flat = block.reshape(clips, 1, frames, patches, width)
    moved = lax.all_to_all(flat, ("fx", "fy"), split_axis=3, concat_axis=1, tiled=True)
    result = moved.reshape(clips, group * frames, columns, width)
    return result


def to_frames(block):
    clips, all_frames, columns, width = block.shape
    group = lax.axis_size(("fx", "fy"))
    frames = all_frames // group
    flat = block.reshape(clips, group, frames, 1, columns, width)
    moved = lax.all_to_all(flat, ("fx", "fy"), split_axis=1, concat_axis=3, tiled=True)
    result = moved.reshape(clips, frames, group * columns, width)
    return result


def project(normed, triple_weight):
    summed = jnp.dot(
        normed,
        lax.all_gather(triple_weight, ("fx", "fy"), axis=0, tiled=True),
        preferred_element_type=jnp.float32,
    )
    return summed.astype(jnp.bfloat16)


def hidden_gradient(hidden, grad_temporal, triple_weight):
    grad_normed = lax.dot_general(
        grad_temporal,
        lax.all_gather(triple_weight, ("fx", "fy"), axis=0, tiled=True),
        (((1,), (1,)), ((), ())),
        preferred_element_type=jnp.float32,
    )
    unused, norm_back = jax.vjp(normalize, hidden.astype(jnp.float32))
    return norm_back(grad_normed)[0].astype(jnp.bfloat16)


def temporal_gradient(temporal, cotangent):
    clips, frames, columns, triple_width = temporal.shape
    ordered = jnp.transpose(temporal, (0, 2, 1, 3)).reshape(clips * columns, frames, triple_width)
    unused, temporal_back = jax.vjp(partial(attention, heads=HEADS), ordered.astype(jnp.float32))
    column_cot = jnp.transpose(cotangent, (0, 2, 1, 3)).reshape(clips * columns, frames, -1)
    grad_columns = temporal_back(column_cot.astype(jnp.float32))[0].astype(jnp.bfloat16)
    grad_columns = grad_columns.reshape(clips, columns, frames, triple_width)
    return jnp.transpose(grad_columns, (0, 2, 1, 3))


def local(hidden_in, spatial_triple, context_grad, out_weight, triple_weight):
    clips, frames, patches, width = hidden_in.shape
    inner = out_weight.shape[0]
    count = clips * frames * patches
    spatial_in = spatial_triple.astype(jnp.float32).reshape(clips * frames, patches, 3 * inner)
    context_f32, spatial_back = jax.vjp(partial(attention, heads=HEADS), spatial_in)
    context = context_f32.astype(jnp.bfloat16).reshape(count, inner)
    mixed = jnp.dot(
        context,
        lax.all_gather(out_weight, ("fx", "fy"), axis=1, tiled=True),
        preferred_element_type=jnp.float32,
    )
    hidden = (hidden_in.reshape(count, width).astype(jnp.float32) + mixed).astype(jnp.bfloat16)
    normed = normalize(hidden.astype(jnp.float32)).astype(jnp.bfloat16)
    temporal = project(normed, triple_weight)
    temporal_cols = to_columns(temporal.reshape(clips, frames, patches, 3 * inner))
    grad_temporal = temporal_gradient(temporal_cols, context_grad)
    grad_back = to_frames(grad_temporal).reshape(count, 3 * inner)
    grad_hidden = hidden_gradient(hidden, grad_back, triple_weight)
    weight_term = lax.dot_general(
        context, grad_hidden, (((0,), (0,)), ((), ())), preferred_element_type=jnp.float32
    )
    weight_part = lax.psum_scatter(weight_term, ("fx", "fy"), scatter_dimension=1, tiled=True)
    weight_total = lax.psum(weight_part, "dp")
    grad_out_weight = weight_total / (clips * lax.axis_size("dp"))
    grad_context = lax.dot_general(
        grad_hidden,
        lax.all_gather(out_weight, ("fx", "fy"), axis=1, tiled=True),
        (((1,), (1,)), ((), ())),
        preferred_element_type=jnp.float32,
    )
    grad_triple = spatial_back(grad_context.reshape(clips * frames, patches, inner))[0].astype(
        jnp.bfloat16
    )
    return (
        grad_triple.reshape(clips, frames, patches, 3 * inner),
        grad_hidden.reshape(clips, frames, patches, width),
        grad_out_weight,
    )


def solution(mesh):
    placed = (
        P("dp", ("fx", "fy"), None, None),
        P("dp", ("fx", "fy"), None, None),
        P("dp", None, ("fx", "fy"), None),
        P(None, ("fx", "fy")),
        P(("fx", "fy"), None),
    )
    return jax.shard_map(
        local,
        mesh=mesh,
        in_specs=placed,
        out_specs=(
            P("dp", ("fx", "fy"), None, None),
            P("dp", ("fx", "fy"), None, None),
            P(None, ("fx", "fy")),
        ),
        check_vma=False,
    )
```

profile of v0, /device:TPU:2, one launch (start us, length us, event | category | flops | bytes accessed | tf_op | source)
XLA Modules:
  0.0 2091.3 jit_solution(7782958751142574501)
XLA Ops:
  7.2 0.7 all-gather.5.cloned.1.call-update
  7.9 0.0 all-gather.7.cloned.1.call-start
  8.0 0.7 all-gather.7.cloned.1.call-update
  8.7 0.0 all-reduce.9.cloned.1.call-start
  8.7 1.3 fusion.19
  10.0 0.8 copy-done.1
  10.8 1.4 convolution_convert_fusion.1
  12.2 313.9 %all-gather.5.cloned.1.call-done = bf16[128,9,576]{2,1,0:T(8,128)(2,1)} async-done(((bf16[1,9,576]{2,1,0:T(8,128)(2,1)}), bf16[128,9,576]{2,1,0:T(8,128)(2,1)}) %all-gather.5.cloned.1.call-update) | async-done | bytes 1327120 | tf_op jit(solution)/shard_map/all_gather | solution.py:94
  326.2 3.0 reshape.239
  329.2 0.7 fusion.20
  329.9 0.2 multiply_reduce_fusion.1
  330.1 316.5 %all-gather.7.cloned.1.call-done = bf16[128,9,1728]{2,1,0:T(8,128)(2,1)} async-done(((bf16[1,9,1728]{2,1,0:T(8,128)(2,1)}), bf16[128,9,1728]{2,1,0:T(8,128)(2,1)}) %all-gather.7.cloned.1.call-update) | async-done | bytes 3981328 | tf_op jit(solution)/shard_map/all_gather | solution.py:58
  646.6 8.3 reshape.241
  654.9 4.6 fusion.2
  659.5 2.4 copy.33
  661.9 0.5 broadcast.125
  662.4 4.3 reduce.8
  666.7 1.5 reshape.243
  668.2 28.5 %all_to_all.8 = bf16[128,2,864]{2,1,0:T(2,128)(2,1)} all-to-all(bf16[128,2,864]{2,1,0:T(2,128)(2,1)S(1)} %reshape.243), channel_id=1, replica_groups=mesh['fx'=8,'fy'=16,'dp'=4] {'fx','fy'}, dimensions={0} | all-to-all | bytes 884736 | tf_op jit(solution)/shard_map/all_to_all | solution.py:40
  696.7 3.2 reshape.244
  699.8 1.8 copy.34
  701.7 1.3 fusion.21
  703.0 0.7 convolution_bitcast_fusion.5
  703.7 1.2 fusion.6
  704.9 0.5 convolution_bitcast_fusion.3
  705.5 0.7 convolution_bitcast_fusion.4
  706.2 0.8 add_convert_fusion.1
  707.0 2.4 copy.38
  709.4 4.3 reduce.9
  713.7 1.5 reshape.245
  715.2 23.6 %all_to_all.9 = bf16[128,2,864]{2,1,0:T(2,128)(2,1)} all-to-all(bf16[128,2,864]{2,1,0:T(2,128)(2,1)S(1)} %reshape.245), channel_id=1, replica_groups=mesh['fx'=8,'fy'=16,'dp'=4] {'fx','fy'}, dimensions={0} | all-to-all | bytes 884736 | tf_op jit(solution)/shard_map/all_to_all | solution.py:50
  738.7 3.2 reshape.246
  741.9 1.8 copy.39
  743.7 3.9 multiply_reduce_fusion
  747.6 0.3 fusion.18
  747.9 2.3 fusion.23
  750.2 1.3 dynamic-slice
  752.2 0.7 fusion.22
  752.9 0.5 multiply_reduce_fusion.2
  753.4 1.2 convolution_bitcast_fusion.2
  754.6 0.5 convolution_bitcast_fusion
  755.1 0.7 convolution_bitcast_fusion.1
  755.8 0.8 add_convert_fusion
  756.7 0.8 fusion.36
  757.5 1300.4 %all-reduce.9.cloned.1.call-done = f32[576,1152]{0,1:T(8,128)} async-done(((f32[576,1152]{0,1:T(8,128)}), f32[576,1152]{0,1:T(8,128)}) %all-reduce.9.cloned.1.call-update) | async-done | bytes 2654224
  2057.9 0.8 constant_dynamic-slice_fusion
  2058.7 25.4 %psum.7 = f32[576,9]{0,1:T(8,128)S(1)} all-reduce(f32[576,9]{0,1:T(8,128)S(1)} %constant_dynamic-slice_fusion), channel_id=1, replica_groups=mesh['fx'=8,'fy'=16,'dp'=4] {'dp'}, use_global_device_ids=true, to_apply=%region_9.0 | all-reduce | flops 5184 | bytes 41472 | tf_op jit(solution)/shard_map/psum | solution.py:108
  2084.1 0.6 broadcast_multiply_fusion
  (21 shorter events, 0.1 us)
Async XLA Ops:
  7.2 695.9 %copy-start = (bf16[1,128,1,576]{1,3,2,0:T(8,128)(2,1)S(1)}, bf16[1,128,1,576]{1,3,2,0:T(8,128)(2,1)}, u32[]{:S(2)}) copy-start(bf16[1,128,1,576]{1,3,2,0:T(8,128)(2,1)} %param.7) | copy-start | bytes 442372
  7.2 319.0 %all-gather.5.cloned.1.call-start = ((), (), s32[]{:S(2)}) async-start(), calls=%async_computation.2 | async-start | bytes 2641920 | tf_op jit(solution)/shard_map/all_gather | solution.py:94
  7.9 638.7 %all-gather.7.cloned.1.call-start = ((), (), s32[]{:S(2)}) async-start(), calls=%async_computation.3 | async-start | bytes 7397376 | tf_op jit(solution)/shard_map/all_gather | solution.py:58
  8.7 2049.2 %all-reduce.9.cloned.1.call-start = ((), (), s32[]{:S(2)}) async-start(), calls=%async_computation.4 | async-start | bytes 5898240
  10.0 0.8 copy-start.1
  10.8 318.4 %copy-start.5 = (bf16[1,1,128,1152]{3,2,1,0:T(8,128)(2,1)S(1)}, bf16[1,1,128,1152]{3,2,1,0:T(8,128)(2,1)}, u32[]{:S(2)}) copy-start(bf16[1,1,128,1152]{3,2,1,0:T(8,128)(2,1)} %param.5) | copy-start | bytes 884740
  701.7 3.3 copy-start.3
  750.2 2.7 copy-start.2
  750.2 2.7 copy-start.4
Sparse Core Ops, SparseCore 0:
  10.1 315.9 all-gather.4
  328.3 318.2 all-gather.6
  750.3 1307.5 all-reduce.8
where the time goes:
time: 2090 us
  waiting for transfers between devices  1930 us (92%)
  blocking collectives  77.4 us (4%)
  local copies, waits for them, and re-layouts  32.4 us (2%)
  matrix products  22.2 us (1%)
    unnamed x4, waiting for transfers between devices  1300 us
    all_gather x1, waiting for transfers between devices, project(): lax.all_gather(triple_weight, ('fx', 'fy'), axis=0, tiled=True)  317 us
    all_gather x1, waiting for transfers between devices, local(): lax.all_gather(out_weight, ('fx', 'fy'), axis=1, tiled=True)  314 us
  transfers between devices with their start and end apart: 3, of which 3 were waited for; matrix products, arithmetic and copies ran while one was open for 1% of the time, Pallas kernels for 0%

commit v1 on v0

v1 whole, which is shorter than its diff:
```python
import math

import numpy as np
import jax
import jax.numpy as jnp
from jax import lax
from jax.experimental import pallas as pl
from jax.experimental.pallas import tpu as pltpu
from jax.sharding import PartitionSpec as P

HEADS = 8
SIZE = 72
INNER = HEADS * SIZE
D = 1152
TOKENS = 128
GX, GY = 8, 16
ROWS = 9
BF = jnp.bfloat16
F32 = jnp.float32
SCALE = 1.0 / math.sqrt(SIZE)
PARAMS = pltpu.CompilerParams(vmem_limit_bytes=48 * 1024 * 1024)

_place = np.arange(D)
_j, _i, _r = _place // 72, (_place // 9) % 8, _place % 9
FEATURE_AT = ((_i * GY + _j) * ROWS + _r).astype(np.int32)
PLACE_OF = np.argsort(FEATURE_AT).astype(np.int32)
_t = np.arange(TOKENS)
ROW_AT = ((_t % 8) * 16 + _t // 8).astype(np.int32)
ROW_BACK = ((_t % 16) * 8 + _t // 16).astype(np.int32)
_c = np.arange(640)
HALF_A = np.where(_c % 40 < 36, (_c // 40) * 72 + _c % 40, -1).astype(np.int32)
HALF_B = np.where(_c % 40 < 36, (_c // 40) * 72 + 36 + _c % 40, -1).astype(np.int32)
_s = np.arange(32)
FIRST_ROWS = ((_s // 8) * 9 + _s % 8).astype(np.int32)
LAST_ROW = np.where(_s % 8 == 0, (_s // 8) * 9 + 8, -1).astype(np.int32)


def dot(a, b, dims):
    return lax.dot_general(a, b, (dims, ((), ())), preferred_element_type=F32)


def nn(a, b):
    return dot(a, b, ((1,), (0,)))


def nt(a, b):
    return dot(a, b, ((1,), (1,)))


def tn(a, b):
    return dot(a, b, ((0,), (0,)))


def pick_columns(rows, source):
    at = lax.broadcasted_iota(jnp.int32, (rows, source.shape[1]), 0)
    return jnp.where(at == source, 1.0, 0.0).astype(BF)


def pick_rows(source, columns):
    at = lax.broadcasted_iota(jnp.int32, (source.shape[0], columns), 1)
    return jnp.where(at == source, 1.0, 0.0).astype(BF)


def stack_heads(x):
    lane = lax.broadcasted_iota(jnp.int32, (1, INNER), 1)
    parts = []
    for h in range(HEADS):
        mask = jnp.where((lane >= h * SIZE) & (lane < (h + 1) * SIZE), 1.0, 0.0).astype(BF)
        parts.append(x * mask)
    return jnp.concatenate(parts, axis=0)


def head_of(x, h):
    return x[:, h * TOKENS:(h + 1) * TOKENS]


def softmax(scores):
    shifted = scores * SCALE
    top = jnp.max(shifted, axis=-1, keepdims=True)
    e = jnp.exp(shifted - top)
    return e / jnp.sum(e, axis=-1, keepdims=True)


def attend(q, k, v):
    scores = nt(q, stack_heads(k))
    weights = [softmax(head_of(scores, h)).astype(BF) for h in range(HEADS)]
    return nn(jnp.concatenate(weights, axis=1), stack_heads(v))


def attend_back(q, k, v, cot):
    stacked_k = stack_heads(k)
    scores = nt(q, stacked_k)
    grad_weights = nt(cot, stack_heads(v))
    weights, grad_scores = [], []
    for h in range(HEADS):
        p = softmax(head_of(scores, h))
        g = head_of(grad_weights, h)
        mean = jnp.sum(p * g, axis=-1, keepdims=True)
        weights.append(p.astype(BF))
        grad_scores.append((p * (g - mean) * SCALE).astype(BF))
    grad_q = nn(jnp.concatenate(grad_scores, axis=1), stacked_k)
    grad_k = tn(jnp.concatenate(grad_scores, axis=0), stack_heads(q))
    grad_v = tn(jnp.concatenate(weights, axis=0), stack_heads(cot))
    return grad_q, grad_k, grad_v


def split_triple(triple):
    return triple[:, :INNER], triple[:, INNER:2 * INNER], triple[:, 2 * INNER:]


def gather_kernel(packed, out_copies, triple_rows, held):
    for i in range(GX):
        held[i * ROWS:(i + 1) * ROWS, :] = packed[i].astype(F32)
    rows = held[...]
    part = rows[:, :INNER].astype(BF)
    for j in range(GY):
        out_copies[j] = part
    triple_rows[...] = rows[:, INNER:].astype(BF)


def context_kernel(triple, hidden_in, feature_at, context, hidden_placed):
    q, k, v = split_triple(triple[...])
    context[...] = attend(q, k, v).astype(BF)
    hidden_placed[...] = nn(hidden_in[...], pick_columns(D, feature_at[...])).astype(BF)


def hidden_kernel(context, hidden_placed, out_rows, row_at, payload):
    ctx = context[...]
    hidden = (hidden_placed[...].astype(F32) + nt(ctx, out_rows[...])).astype(BF)
    turn = pick_rows(row_at[...], TOKENS)
    payload[:, :D] = nn(turn, hidden).astype(BF)
    payload[:, D:] = nn(turn, ctx).astype(BF)


def temporal_kernel(payload, weight, cotangent, row_at, half_a, half_b, message):
    hidden = payload[:, :D].astype(F32)
    ctx = payload[:, D:]
    centred = hidden - jnp.mean(hidden, axis=-1, keepdims=True)
    scale = lax.rsqrt(jnp.mean(centred * centred, axis=-1, keepdims=True) + 1e-06)
    normal = centred * scale
    w = weight[...]
    triple = nn(normal.astype(BF), w).astype(BF)
    q, k, v = split_triple(triple)
    grads = attend_back(q, k, v, cotangent[...])
    grad_triple = jnp.concatenate(grads, axis=1).astype(BF)
    grad_normal = nt(grad_triple, w)
    along = jnp.mean(grad_normal * normal, axis=-1, keepdims=True)
    level = jnp.mean(grad_normal, axis=-1, keepdims=True)
    grad_hidden = (scale * (grad_normal - level - normal * along)).astype(BF)
    turned = nn(pick_rows(row_at[...], TOKENS), grad_hidden)
    halves = jnp.concatenate(
        [
            nn(grad_hidden, pick_columns(D, half_a[...])).astype(BF),
            nn(grad_hidden, pick_columns(D, half_b[...])).astype(BF),
        ],
        axis=0,
    )
    ctx32 = ctx.astype(F32)
    blank = jnp.zeros((TOKENS, INNER), F32)
    sides = jnp.concatenate(
        [
            jnp.concatenate([ctx32, blank], axis=1),
            jnp.concatenate([blank, ctx32], axis=1),
        ],
        axis=0,
    ).astype(BF)
    term = tn(halves, sides)
    for j in range(GY):
        message[j] = jnp.concatenate(
            [term[j * 40:(j + 1) * 40], turned[j * 8:(j + 1) * 8]], axis=0
        ).astype(BF)


def turn_kernel(received, row_back, first_rows, last_row, message):
    total = received[0].astype(F32)
    parts = [total[40:]]
    total = total[:40]
    for j in range(1, GY):
        one = received[j].astype(F32)
        parts.append(one[40:])
        total = total + one[:40]
    grad = jnp.concatenate(parts, axis=0).astype(BF)
    turned = nn(pick_rows(row_back[...], TOKENS), grad)
    first = pick_rows(first_rows[...], 40)
    last = pick_rows(last_row[...], 40)
    for half in range(2):
        part = total[:, half * INNER:(half + 1) * INNER].astype(BF)
        both = jnp.concatenate([nn(first, part), nn(last, part)], axis=1)
        for low in range(4):
            i = half * 4 + low
            message[i] = jnp.concatenate(
                [turned[i * 16:(i + 1) * 16], both[low * 8:(low + 1) * 8]], axis=0
            ).astype(BF)


def sum_kernel(received, total):
    s = received[0, 16:, :].astype(F32)
    for i in range(1, GX):
        s = s + received[i, 16:, :].astype(F32)
    total[:8] = s[:, :INNER]
    total[8:] = s[:, INNER:]


def final_kernel(received, out_rows, triple, place_of, grad_triple, grad_hidden):
    grad = jnp.concatenate([received[i, :16, :] for i in range(GX)], axis=0)
    grad_hidden[...] = nn(grad, pick_columns(D, place_of[...])).astype(BF)
    cot = nn(grad, out_rows[...]).astype(BF)
    q, k, v = split_triple(triple[...])
    grad_triple[...] = jnp.concatenate(attend_back(q, k, v, cot), axis=1).astype(BF)


def call(kernel, name, outs, *args, scratch=()):
    many = isinstance(outs, list)
    shapes = [jax.ShapeDtypeStruct(s, t) for s, t in (outs if many else [outs])]
    return pl.pallas_call(
        kernel,
        out_shape=shapes if many else shapes[0],
        in_specs=[pl.BlockSpec(memory_space=pltpu.VMEM)] * len(args),
        out_specs=(
            [pl.BlockSpec(memory_space=pltpu.VMEM)] * len(shapes)
            if many
            else pl.BlockSpec(memory_space=pltpu.VMEM)
        ),
        scratch_shapes=list(scratch),
        compiler_params=PARAMS,
        name=name,
    )(*args)


def exchange(x, axis):
    return lax.all_to_all(x, axis, 0, 0, tiled=True)


def local(hidden_in, spatial_triple, context_grad, out_weight, triple_weight):
    hidden_in = hidden_in.reshape(TOKENS, D)
    spatial = spatial_triple.reshape(TOKENS, 3 * INNER)
    cotangent = context_grad.reshape(TOKENS, INNER)

    packed = jnp.concatenate([out_weight.T, triple_weight], axis=1)[None]
    packed = lax.all_gather(packed, "fx", axis=0, tiled=True)
    out_copies, triple_rows = call(
        gather_kernel,
        "gather_weights",
        [((GY, 72, INNER), BF), ((72, 3 * INNER), BF)],
        packed,
        scratch=[pltpu.VMEM((72, 4 * INNER), F32)],
    )
    weight = lax.all_gather(triple_rows, "fy", axis=0, tiled=True)
    spatial, hidden_in, cotangent, out_copies = lax.optimization_barrier(
        (spatial, hidden_in, cotangent, out_copies)
    )
    context, hidden_placed = call(
        context_kernel,
        "spatial_context",
        [((TOKENS, INNER), BF), ((TOKENS, D), BF)],
        spatial,
        hidden_in,
        FEATURE_AT[None],
    )
    out_rows = exchange(out_copies, "fy").reshape(D, INNER)
    payload = call(
        hidden_kernel,
        "hidden",
        ((TOKENS, D + INNER), BF),
        context,
        hidden_placed,
        out_rows,
        ROW_AT[:, None],
    )
    payload = exchange(payload.reshape(GY, GX, D + INNER), "fy")
    payload = exchange(jnp.transpose(payload, (1, 0, 2)), "fx").reshape(TOKENS, D + INNER)
    message = call(
        temporal_kernel,
        "temporal_back",
        ((GY, 48, D), BF),
        payload,
        weight,
        cotangent,
        ROW_AT[:, None],
        HALF_A[None],
        HALF_B[None],
    )
    message = exchange(message, "fy")
    message = call(
        turn_kernel,
        "turn",
        ((GX, 24, D), BF),
        message,
        ROW_BACK[:, None],
        FIRST_ROWS[:, None],
        LAST_ROW[:, None],
    )
    message = exchange(message, "fx")
    part = call(sum_kernel, "weight_sum", ((16, INNER), F32), message)
    parts = lax.all_gather(part[None, :ROWS], "dp", axis=0, tiled=True)
    grad_out_weight = (jnp.sum(parts, axis=0) / lax.axis_size("dp")).T
    grad_triple, grad_hidden = call(
        final_kernel,
        "spatial_back",
        [((TOKENS, 3 * INNER), BF), ((TOKENS, D), BF)],
        message,
        out_rows,
        spatial,
        PLACE_OF[None],
    )
    return (
        grad_triple.reshape(1, 1, TOKENS, 3 * INNER),
        grad_hidden.reshape(1, 1, TOKENS, D),
        grad_out_weight,
    )


def solution(mesh):
    placed = (
        P("dp", ("fx", "fy"), None, None),
        P("dp", ("fx", "fy"), None, None),
        P("dp", None, ("fx", "fy"), None),
        P(None, ("fx", "fy")),
        P(("fx", "fy"), None),
    )
    return jax.shard_map(
        local,
        mesh=mesh,
        in_specs=placed,
        out_specs=(
            P("dp", ("fx", "fy"), None, None),
            P("dp", ("fx", "fy"), None, None),
            P(None, ("fx", "fy")),
        ),
        check_vma=False,
    )
```

time: 2090 us -> 190 us (0.09)
  waiting for transfers between devices: 1930 us -> 30.2 us
  blocking collectives: 77.4 us -> 118 us
  local copies, waits for them, and re-layouts: 32.4 us -> 1.5 us
  matrix products: 22.2 us -> 0 us
    unnamed x4 -> x1, waiting for transfers between devices: 1300 us -> 0.02 us
    all_gather x2 -> x1, waiting for transfers between devices: 630 us -> 8.95 us  [local(): weight = lax.all_gather(triple_rows, 'fy', axis=0, tiled=True)]
    all_gather x0 -> x2, blocking collectives: none -> 38.1 us  [the longest x1 21.9 us: local(): parts = lax.all_gather(part[None, :ROWS], 'dp', axis=0, tiled=True)]
    all_to_all x2 -> x4, blocking collectives: 52.1 us -> 79.9 us  [exchange(): return lax.all_to_all(x, axis, 0, 0, tiled=True)]
    psum x1 -> x0, blocking collectives: 25.4 us -> none  [local(): weight_total = lax.psum(weight_part, 'dp')]
    unnamed x21 -> x26, local copies, waits for them, and re-layouts: 24 us -> 1.42 us
    dot_general x16 -> x0, matrix products: 22.2 us -> none  [the longest x6 5.1 us: attention(): jnp.einsum('bqhe,bkhe->bhqk', query, keys, precision=lax.Precision.HIGHEST)]
    all_to_all x0 -> x1, waiting for transfers between devices: none -> 21.2 us  [exchange(): return lax.all_to_all(x, axis, 0, 0, tiled=True)]
  transfers between devices with their start and end apart: 3 -> 2, of which waited for: 3 -> 2; matrix products, arithmetic and copies ran while one was open for 1% -> 0% of each run, Pallas kernels for 0% -> 1%
where the time goes in v1:
time: 190 us; the launch traced here: 189 us
  blocking collectives  118 us (62%)
  waiting for transfers between devices  30.2 us (16%)
  Pallas kernels  15.1 us (8%)
  between operations  14.2 us (7%)
  starting transfers between devices  8.58 us (5%)
    all_to_all x4, blocking collectives, exchange(): return lax.all_to_all(x, axis, 0, 0, tiled=True)  79.9 us
    all_gather x1, blocking collectives, local(): parts = lax.all_gather(part[None, :ROWS], 'dp', axis=0, tiled=True)  21.9 us
    all_to_all x1, waiting for transfers between devices, exchange(): return lax.all_to_all(x, axis, 0, 0, tiled=True)  21.2 us
    all_gather x1, blocking collectives, local(): packed = lax.all_gather(packed, 'fx', axis=0, tiled=True)  16.2 us
    pallas_call x7, Pallas kernels, call(): pl.pallas_call(kernel, out_shape=shapes if many else shapes[0], in_specs=...  15.1 us
    all_gather x1, waiting for transfers between devices, local(): weight = lax.all_gather(triple_rows, 'fy', axis=0, tiled=True)  8.95 us
    all_to_all x1, starting transfers between devices, exchange(): return lax.all_to_all(x, axis, 0, 0, tiled=True)  8.55 us
  transfers between devices with their start and end apart: 2, of which 2 were waited for; matrix products, arithmetic and copies ran while one was open for 0% of the time, Pallas kernels for 1%

profile of v1, /device:TPU:2, one launch (start us, length us, event | category | flops | bytes accessed | tf_op | source)
XLA Modules:
  0.0 189.2 jit_solution(17310617200799052694)
XLA Ops:
  7.2 0.0 copy-start.10
  7.2 0.0 copy-start.9
  7.2 0.0 all-gather.6.cloned.1.call-start
  7.2 1.0 maximum_bitcast_fusion
  8.2 16.2 %all-gather.2.packed = bf16[8,9,2304]{2,1,0:T(8,128)(2,1)S(1)} all-gather(bf16[1,9,2304]{2,1,0:T(8,128)(2,1)S(1)} %maximum_bitcast_fusion), channel_id=2, replica_groups=mesh['fx'=8,'fy'=16,'dp'=4] {'fx'}, dimensions={0}, use_global_device_ids=true | all-gather | bytes 373248 | tf_op jit(solution)/shard_map/all_gather | solution.py:240
  24.4 1.4 gather_weights.1
  25.8 0.0 all-gather.6.cloned.1.call-update
  25.8 0.0 copy-done.10
  25.8 0.2 copy.26
  26.0 0.0 copy-done.9
  26.0 0.0 copy-start
  26.0 0.0 copy-start.5
  26.0 0.2 copy.25
  26.3 0.0 copy-start.1
  26.3 8.5 %all-to-all-start = ((bf16[16,72,576]{2,1,0:T(8,128)(2,1)}), bf16[16,72,576]{2,1,0:T(8,128)(2,1)S(1)}, u32[]{:S(2)}, u32[]{:S(2)}) async-start(bf16[16,72,576]{2,1,0:T(8,128)(2,1)} %get-tuple-element.18), calls=%async_computation | async-start | bytes 2949120 | tf_op jit(solution)/shard_map/all_to_all | solution.py:231
  34.8 0.0 copy-done
  34.8 0.0 copy-done.5
  34.8 1.8 spatial_context.1
  36.7 21.2 %all-to-all-done = bf16[16,72,576]{2,1,0:T(8,128)(2,1)S(1)} async-done(((bf16[16,72,576]{2,1,0:T(8,128)(2,1)}), bf16[16,72,576]{2,1,0:T(8,128)(2,1)S(1)}, u32[]{:S(2)}, u32[]{:S(2)}) %all-to-all-start) | async-done | bytes 1327136 | tf_op jit(solution)/shard_map/all_to_all | solution.py:231
  57.9 0.0 copy-done.1
  57.9 0.8 hidden.1
  58.7 0.0 copy-start.7
  58.7 0.0 copy-start.8
  58.7 15.8 %all_to_all.25 = bf16[16,8,1728]{2,1,0:T(8,128)(2,1)S(1)} all-to-all(bf16[16,8,1728]{2,1,0:T(8,128)(2,1)S(1)} %bitcast.21), channel_id=1, replica_groups=mesh['fx'=8,'fy'=16,'dp'=4] {'fy'}, dimensions={0} | all-to-all | bytes 884736 | tf_op jit(solution)/shard_map/all_to_all | solution.py:231
  74.5 0.1 copy.27
  74.6 16.8 %all_to_all.26 = bf16[8,16,1728]{2,1,0:T(8,128)(2,1)S(1)} all-to-all(bf16[8,16,1728]{2,1,0:T(8,128)(2,1)S(1)} %copy.27), channel_id=1, replica_groups=mesh['fx'=8,'fy'=16,'dp'=4] {'fx'}, dimensions={0} | all-to-all | bytes 884736 | tf_op jit(solution)/shard_map/all_to_all | solution.py:231
  91.4 9.0 %all-gather.6.cloned.1.call-done.weight = bf16[1152,1728]{1,0:T(8,128)(2,1)} async-done(((bf16[72,1728]{1,0:T(8,128)(2,1)}), bf16[1152,1728]{1,0:T(8,128)(2,1)}) %all-gather.6.cloned.1.call-update) | async-done | bytes 3981328 | tf_op jit(solution)/shard_map/all_gather | solution.py:248
  100.3 0.0 copy-done.7
  100.3 0.0 copy-done.8
  100.3 7.8 %temporal_back.1 = bf16[16,48,1152]{2,1,0:T(8,128)(2,1)S(1)} custom-call(bf16[128,1728]{1,0:T(8,128)(2,1)S(1)} %bitcast.20, bf16[1152,1728]{1,0:T(8,128)(2,1)} %all-gather.6.cloned.1.call-done.weight, bf16[128,576]{1,0:T(8,128)(2,1)S(1)} %bitcast.22, s32[128,1]{1,0:T(8,128)S(1)} %copy-done.1, s32[1,640]{1,0:T(1,128)S(1)} %copy-done.8, s32[1,640]{1,0:T(1,128)S(1)} %copy-done.7), custom_call_target="tpu_custom_call" | custom-call | tf_op jit(solution)/shard_map/temporal_back/pallas_call | solution.py:215
  108.1 0.0 copy-start.2
  108.2 0.0 copy-start.3
  108.2 0.0 copy-start.4
  108.2 29.2 %all_to_all.27.received = bf16[16,48,1152]{2,1,0:T(8,128)(2,1)S(1)} all-to-all(bf16[16,48,1152]{2,1,0:T(8,128)(2,1)S(1)} %temporal_back.1), channel_id=1, replica_groups=mesh['fx'=8,'fy'=16,'dp'=4] {'fy'}, dimensions={0} | all-to-all | bytes 3538944 | tf_op jit(solution)/shard_map/all_to_all | solution.py:231
  137.3 0.0 copy-done.2
  137.3 0.0 copy-done.3
  137.3 0.0 copy-done.4
  137.3 0.0 copy-start.6
  137.4 0.5 turn.1
  137.9 18.2 %all_to_all.28.received = bf16[8,24,1152]{2,1,0:T(8,128)(2,1)S(1)} all-to-all(bf16[8,24,1152]{2,1,0:T(8,128)(2,1)S(1)} %turn.1), channel_id=1, replica_groups=mesh['fx'=8,'fy'=16,'dp'=4] {'fx'}, dimensions={0} | all-to-all | bytes 884736 | tf_op jit(solution)/shard_map/all_to_all | solution.py:231
  156.1 0.1 weight_sum.1
  156.2 0.0 copy-done.6
  156.2 2.6 %spatial_back.1 = (bf16[128,1728]{1,0:T(8,128)(2,1)S(1)}, bf16[128,1152]{1,0:T(8,128)(2,1)}) custom-call(bf16[8,24,1152]{2,1,0:T(8,128)(2,1)S(1)} %all_to_all.28.received, bf16[1152,576]{1,0:T(8,128)(2,1)S(1)} %bitcast.17, bf16[128,1728]{1,0:T(8,128)(2,1)S(1)} %bitcast.19, s32[1,1152]{1,0:T(1,128)S(1)} %copy-done.6), custom_call_target="tpu_custom_call" | custom-call | tf_op jit(solution)/shard_map/spatial_back/pallas_call | solution.py:215
  158.8 1.0 copy.28
  159.8 21.9 %all-gather.3 = f32[4,9,576]{2,1,0:T(8,128)S(1)} all-gather(f32[1,9,576]{2,1,0:T(8,128)S(1)} %slice_bitcast_fusion), channel_id=3, replica_groups=mesh['fx'=8,'fy'=16,'dp'=4] {'dp'}, dimensions={0}, use_global_device_ids=true | all-gather | bytes 103680 | tf_op jit(solution)/shard_map/all_gather | solution.py:295
  181.7 0.6 multiply_bitcast_fusion
  (2 shorter events, 0.0 us)
Async XLA Ops:
  7.2 18.7 %copy-start.10 = (bf16[1,128,1,576]{1,3,2,0:T(8,128)(2,1)S(1)}, bf16[1,128,1,576]{1,3,2,0:T(8,128)(2,1)}, u32[]{:S(2)}) copy-start(bf16[1,128,1,576]{1,3,2,0:T(8,128)(2,1)} %param.16) | copy-start | bytes 442372
  7.2 18.8 %copy-start.9 = (bf16[1,1,128,1728]{2,3,1,0:T(8,128)(2,1)S(1)}, bf16[1,1,128,1728]{2,3,1,0:T(8,128)(2,1)}, u32[]{:S(2)}) copy-start(bf16[1,1,128,1728]{2,3,1,0:T(8,128)(2,1)} %param.15) | copy-start | bytes 1327108
  7.2 93.1 %all-gather.6.cloned.1.call-start = ((), (), s32[]{:S(2)}) async-start(), calls=%async_computation.5 | async-start | bytes 4386816 | tf_op jit(solution)/shard_map/all_gather | solution.py:248
  26.0 8.8 %copy-start = (bf16[1,1,128,1152]{3,2,1,0:T(8,128)(2,1)S(1)}, bf16[1,1,128,1152]{3,2,1,0:T(8,128)(2,1)}, u32[]{:S(2)}) copy-start(bf16[1,1,128,1152]{3,2,1,0:T(8,128)(2,1)} %param.14) | copy-start | bytes 884740
  26.0 8.8 %copy-start.5 = (s32[1,1152]{1,0:T(1,128)S(1)}, s32[1,1152]{1,0:T(1,128)}, u32[]{:S(2)}) copy-start(s32[1,1152]{1,0:T(1,128)} %constant.21.clone.feature_at) | copy-start | bytes 13828
  26.3 31.6 %copy-start.1 = (s32[128,1]{1,0:T(8,128)S(1)}, s32[128,1]{1,0:T(8,128)}, u32[]{:S(2)}) copy-start(s32[128,1]{1,0:T(8,128)} %constant.22.clone.row_at) | copy-start | bytes 1540
  26.3 31.6 %all-to-all-start = ((bf16[16,72,576]{2,1,0:T(8,128)(2,1)}), bf16[16,72,576]{2,1,0:T(8,128)(2,1)S(1)}, u32[]{:S(2)}, u32[]{:S(2)}) async-start(bf16[16,72,576]{2,1,0:T(8,128)(2,1)} %get-tuple-element.18), calls=%async_computation | async-start | bytes 2949120 | tf_op jit(solution)/shard_map/all_to_all | solution.py:231
  58.7 41.6 %copy-start.7 = (s32[1,640]{1,0:T(1,128)S(1)}, s32[1,640]{1,0:T(1,128)}, u32[]{:S(2)}) copy-start(s32[1,640]{1,0:T(1,128)} %constant.24.clone.half_b) | copy-start | bytes 7684
  58.7 41.6 %copy-start.8 = (s32[1,640]{1,0:T(1,128)S(1)}, s32[1,640]{1,0:T(1,128)}, u32[]{:S(2)}) copy-start(s32[1,640]{1,0:T(1,128)} %constant.23.clone.half_a) | copy-start | bytes 7684
  108.1 29.2 %copy-start.2 = (s32[128,1]{1,0:T(8,128)S(1)}, s32[128,1]{1,0:T(8,128)}, u32[]{:S(2)}) copy-start(s32[128,1]{1,0:T(8,128)} %constant.25.clone.row_back) | copy-start | bytes 1540
  108.2 29.2 %copy-start.3 = (s32[32,1]{1,0:T(8,128)S(1)}, s32[32,1]{1,0:T(8,128)}, u32[]{:S(2)}) copy-start(s32[32,1]{1,0:T(8,128)} %constant.27.clone.last_row) | copy-start | bytes 388
  108.2 29.2 %copy-start.4 = (s32[32,1]{1,0:T(8,128)S(1)}, s32[32,1]{1,0:T(8,128)}, u32[]{:S(2)}) copy-start(s32[32,1]{1,0:T(8,128)} %constant.26.clone.first_rows) | copy-start | bytes 388
  137.3 18.8 %copy-start.6 = (s32[1,1152]{1,0:T(1,128)S(1)}, s32[1,1152]{1,0:T(1,128)}, u32[]{:S(2)}) copy-start(s32[1,1152]{1,0:T(1,128)} %constant.28.clone.place_of) | copy-start | bytes 13828
Sparse Core Ops, SparseCore 0:
  25.9 74.3 all-gather.5

commit v2 on v1

v2 whole, which is shorter than its diff:
```python
import math

import numpy as np
import jax
import jax.numpy as jnp
from jax import lax
from jax.experimental import pallas as pl
from jax.experimental.pallas import tpu as pltpu
from jax.sharding import PartitionSpec as P

HEADS = 8
SIZE = 72
INNER = HEADS * SIZE
D = 1152
TOKENS = 128
GX, GY = 8, 16
CLIP_GROUPS = 4
ROWS = 9
PART, REST = 864, 288
BF = jnp.bfloat16
F32 = jnp.float32
SCALE = 1.0 / math.sqrt(SIZE)
PARAMS = pltpu.CompilerParams(vmem_limit_bytes=48 * 1024 * 1024)

_place = np.arange(D)
_j, _i, _r = _place // 72, (_place // 9) % 8, _place % 9
FEATURE_AT = ((_i * GY + _j) * ROWS + _r).astype(np.int32)
PLACE_OF = np.argsort(FEATURE_AT).astype(np.int32)
_t = np.arange(TOKENS)
ROW_AT = ((_t % 8) * 16 + _t // 8).astype(np.int32)
ROW_BACK = ((_t % 16) * 8 + _t // 16).astype(np.int32)


def dot(a, b, dims):
    return lax.dot_general(a, b, (dims, ((), ())), preferred_element_type=F32)


def nn(a, b):
    return dot(a, b, ((1,), (0,)))


def nt(a, b):
    return dot(a, b, ((1,), (1,)))


def tn(a, b):
    return dot(a, b, ((0,), (0,)))


def pick_columns(rows, source):
    at = lax.broadcasted_iota(jnp.int32, (rows, source.shape[1]), 0)
    return jnp.where(at == source, 1.0, 0.0).astype(BF)


def pick_rows(source, columns):
    at = lax.broadcasted_iota(jnp.int32, (source.shape[0], columns), 1)
    return jnp.where(at == source, 1.0, 0.0).astype(BF)


def stack_heads(x):
    lane = lax.broadcasted_iota(jnp.int32, (1, INNER), 1)
    parts = []
    for h in range(HEADS):
        mask = jnp.where((lane >= h * SIZE) & (lane < (h + 1) * SIZE), 1.0, 0.0).astype(BF)
        parts.append(x * mask)
    return jnp.concatenate(parts, axis=0)


def head_of(x, h):
    return x[:, h * TOKENS:(h + 1) * TOKENS]


def softmax(scores):
    shifted = scores * SCALE
    top = jnp.max(shifted, axis=-1, keepdims=True)
    e = jnp.exp(shifted - top)
    return e / jnp.sum(e, axis=-1, keepdims=True)


def attend(q, k, v):
    scores = nt(q, stack_heads(k))
    weights = [softmax(head_of(scores, h)).astype(BF) for h in range(HEADS)]
    return nn(jnp.concatenate(weights, axis=1), stack_heads(v))


def attend_back(q, k, v, cot):
    stacked_k = stack_heads(k)
    scores = nt(q, stacked_k)
    grad_weights = nt(cot, stack_heads(v))
    weights, grad_scores = [], []
    for h in range(HEADS):
        p = softmax(head_of(scores, h))
        g = head_of(grad_weights, h)
        mean = jnp.sum(p * g, axis=-1, keepdims=True)
        weights.append(p.astype(BF))
        grad_scores.append((p * (g - mean) * SCALE).astype(BF))
    grad_q = nn(jnp.concatenate(grad_scores, axis=1), stacked_k)
    grad_k = tn(jnp.concatenate(grad_scores, axis=0), stack_heads(q))
    grad_v = tn(jnp.concatenate(weights, axis=0), stack_heads(cot))
    return grad_q, grad_k, grad_v


def split_triple(triple):
    return triple[:, :INNER], triple[:, INNER:2 * INNER], triple[:, 2 * INNER:]


def spread(x, held):
    for t in range(x.shape[1] // 128):
        held[:, t, :] = x[:, t * 128:(t + 1) * 128]


def collect(held, first, count):
    return jnp.concatenate([held[:, t, :] for t in range(first, first + count)], axis=1)


def context_kernel(triple, hidden_in, tokens, held):
    q, k, v = split_triple(triple[...])
    context = attend(q, k, v)
    blank = jnp.zeros((TOKENS, 16 * 128 - D - INNER), F32)
    spread(jnp.concatenate([hidden_in[...].astype(F32), context, blank], axis=1), held)
    tokens[...] = held[...].astype(BF)


def forward_kernel(core, packed, copies, held):
    for i in range(GX):
        held[i * ROWS:(i + 1) * ROWS, :] = packed[i].astype(F32)
    part = jnp.where(core[0] == 0, held[:, :D], held[:, D:]).astype(BF)
    for j in range(GY):
        copies[j] = part


def place_kernel(core, near, tokens, feature_at, placed, held):
    held[...] = tokens[...].astype(F32)
    hidden_in = collect(held, 0, 9).astype(BF)
    ctx32 = collect(held, 9, 5)[:, :INNER]
    half = jnp.where(core[0] == 0, ctx32[:, :REST], ctx32[:, REST:]).astype(BF)
    placed[...] = nn(hidden_in, pick_columns(D, feature_at[...])) + nt(half, near[:, PART:])


def temporal_kernel(
    core, near, far, placed, tokens, cotangent, row_at, message, out_rows, held
):
    first = core[0] == 0
    w_near = near[...]
    w_far = far[...]
    near_out = w_near[:, PART:]
    far_out = w_far[:, PART:]
    out_rows[:, :REST] = jnp.where(first, near_out, far_out)
    out_rows[:, REST:] = jnp.where(first, far_out, near_out)
    held[...] = tokens[:, 8:, :].astype(F32)
    ctx32 = collect(held, 1, 5)[:, :INNER]
    half = jnp.where(first, ctx32[:, REST:], ctx32[:, :REST]).astype(BF)

    hidden = (placed[...] + nt(half, far_out)).astype(BF).astype(F32)
    centred = hidden - jnp.mean(hidden, axis=-1, keepdims=True)
    scale = lax.rsqrt(jnp.mean(centred * centred, axis=-1, keepdims=True) + 1e-06)
    normal = centred * scale
    normed = normal.astype(BF)
    t_near = nn(normed, w_near)[:, :PART]
    t_far = nn(normed, w_far)[:, :PART]
    triple = jnp.concatenate(
        [jnp.where(first, t_near, t_far), jnp.where(first, t_far, t_near)], axis=1
    ).astype(BF)
    q, k, v = split_triple(triple)
    grads = jnp.concatenate(attend_back(q, k, v, cotangent[...]), axis=1)
    blank = jnp.zeros((TOKENS, REST), F32)
    left = jnp.concatenate([grads[:, :PART], blank], axis=1)
    right = jnp.concatenate([grads[:, PART:], blank], axis=1)
    grad_normal = nt(jnp.where(first, left, right).astype(BF), w_near) + nt(
        jnp.where(first, right, left).astype(BF), w_far
    )
    along = jnp.mean(grad_normal * normal, axis=-1, keepdims=True)
    level = jnp.mean(grad_normal, axis=-1, keepdims=True)
    grad_hidden = (scale * (grad_normal - level - normal * along)).astype(BF)
    turned = nn(pick_rows(row_at[...], TOKENS), grad_hidden)
    low, high = turned[:, :INNER], turned[:, INNER:]
    term = tn(grad_hidden, ctx32.astype(BF))
    for j in range(GY):
        message[j] = jnp.concatenate(
            [
                low[j * 8:(j + 1) * 8],
                high[j * 8:(j + 1) * 8],
                term[j * 72:(j + 1) * 72],
            ],
            axis=0,
        ).astype(BF)


def turn_kernel(received, row_back, message, held):
    one = received[0].astype(F32)
    total, low, high = one[16:], [one[:8]], [one[8:16]]
    for j in range(1, GY):
        one = received[j].astype(F32)
        total = total + one[16:]
        low.append(one[:8])
        high.append(one[8:16])
    held[:72, :] = total
    held[72:, :] = jnp.zeros((8, INNER), F32)
    turn = pick_rows(row_back[...], TOKENS)
    low = nn(turn, jnp.concatenate(low, axis=0).astype(BF)).astype(BF)
    high = nn(turn, jnp.concatenate(high, axis=0).astype(BF)).astype(BF)
    for i in range(GX):
        message[i, :16, :INNER] = low[i * 16:(i + 1) * 16]
        message[i, :16, INNER:] = high[i * 16:(i + 1) * 16]
        at = i * ROWS
        message[i, 16:, :INNER] = held[at:at + 8, :].astype(BF)
        message[i, 16:, INNER:] = held[at + 8:at + 16, :].astype(BF)


def sum_kernel(received, total):
    s = received[0, 16:, :].astype(F32)
    for i in range(1, GX):
        s = s + received[i, 16:, :].astype(F32)
    total[0, :8] = s[:, :INNER]
    total[0, 8:] = s[:1, INNER:]


def final_kernel(received, out_rows, triple, place_of, grad_triple, grad_hidden):
    grad = received[:, :16, :].reshape(TOKENS, D)
    grad_hidden[...] = nn(grad, pick_columns(D, place_of[...])).astype(BF)
    cot = nn(grad, out_rows[...]).astype(BF)
    q, k, v = split_triple(triple[...])
    grad_triple[...] = jnp.concatenate(attend_back(q, k, v, cot), axis=1).astype(BF)


def call(kernel, name, outs, *args, scratch=()):
    many = isinstance(outs, list)
    shapes = [jax.ShapeDtypeStruct(s, t) for s, t in (outs if many else [outs])]
    return pl.pallas_call(
        kernel,
        out_shape=shapes if many else shapes[0],
        in_specs=[
            pl.BlockSpec(memory_space=pltpu.SMEM if a.ndim == 1 else pltpu.VMEM) for a in args
        ],
        out_specs=(
            [pl.BlockSpec(memory_space=pltpu.VMEM)] * len(shapes)
            if many
            else pl.BlockSpec(memory_space=pltpu.VMEM)
        ),
        scratch_shapes=list(scratch),
        compiler_params=PARAMS,
        name=name,
    )(*args)


def exchange(x, axis):
    return lax.all_to_all(x, axis, 0, 0, tiled=True)


def local(hidden_in, spatial_triple, context_grad, out_weight, triple_weight):
    hidden_in = hidden_in.reshape(TOKENS, D)
    spatial = spatial_triple.reshape(TOKENS, 3 * INNER)
    cotangent = context_grad.reshape(TOKENS, INNER)

    core = (lax.axis_index("fx") % 2).astype(jnp.int32)[None]
    out_t = out_weight.T
    packed = jnp.concatenate(
        [triple_weight[:, :PART], out_t[:, :REST], triple_weight[:, PART:], out_t[:, REST:]],
        axis=1,
    )
    packed = lax.all_gather(packed[None], "fx", axis=0, tiled=True)
    slabs = (TOKENS, 16, 128)
    held = pltpu.VMEM(slabs, F32)
    tokens = call(
        context_kernel, "spatial_context", (slabs, BF), spatial, hidden_in, scratch=[held]
    )
    tokens = exchange(tokens, ("fx", "fy"))
    packed, tokens = lax.optimization_barrier((packed, tokens))
    near = call(
        forward_kernel,
        "forward",
        ((GY, 72, D), BF),
        core,
        packed,
        scratch=[pltpu.VMEM((72, 2 * D), F32)],
    )
    near = exchange(near, "fy").reshape(D, D)
    far = lax.ppermute(near, "fx", [(i, i ^ 1) for i in range(GX)])
    placed = call(
        place_kernel,
        "hidden_near",
        ((TOKENS, D), F32),
        core,
        near,
        tokens,
        FEATURE_AT[None],
        scratch=[held],
    )
    message, out_rows = call(
        temporal_kernel,
        "temporal_back",
        [((GY, 88, INNER), BF), ((D, INNER), BF)],
        core,
        near,
        far,
        placed,
        tokens,
        cotangent,
        ROW_AT[:, None],
        scratch=[pltpu.VMEM((TOKENS, 8, 128), F32)],
    )
    message = exchange(message, "fy")
    message = call(
        turn_kernel,
        "turn",
        ((GX, 24, D), BF),
        message,
        ROW_BACK[:, None],
        scratch=[pltpu.VMEM((80, INNER), F32)],
    )
    message = exchange(message, "fx")
    total = call(sum_kernel, "weight_sum", ((1, ROWS, INNER), F32), message)
    totals = lax.all_gather(total, "dp", axis=0, tiled=True)
    grad_triple, grad_hidden = call(
        final_kernel,
        "spatial_back",
        [((TOKENS, 3 * INNER), BF), ((TOKENS, D), BF)],
        message,
        out_rows,
        spatial,
        PLACE_OF[None],
    )
    grad_out_weight = (jnp.sum(totals, axis=0) / CLIP_GROUPS).T
    return (
        grad_triple.reshape(1, 1, TOKENS, 3 * INNER),
        grad_hidden.reshape(1, 1, TOKENS, D),
        grad_out_weight,
    )


def solution(mesh):
    placed = (
        P("dp", ("fx", "fy"), None, None),
        P("dp", ("fx", "fy"), None, None),
        P("dp", None, ("fx", "fy"), None),
        P(None, ("fx", "fy")),
        P(("fx", "fy"), None),
    )
    return jax.shard_map(
        local,
        mesh=mesh,
        in_specs=placed,
        out_specs=(
            P("dp", ("fx", "fy"), None, None),
            P("dp", ("fx", "fy"), None, None),
            P(None, ("fx", "fy")),
        ),
        check_vma=False,
    )
```

time: 190 us -> 174 us (0.916)
  waiting for transfers between devices: 30.2 us -> 2.38 us
  blocking collectives: 118 us -> 134 us
  between operations: 14.2 us -> 0.8 us
  starting transfers between devices: 8.58 us -> 14.9 us
  local copies, waits for them, and re-layouts: 1.5 us -> 4.69 us
    all_to_all x1, waiting for transfers between devices: 21.2 us -> 0.01 us  [exchange(): return lax.all_to_all(x, axis, 0, 0, tiled=True)]
    all_gather x1 -> x0, waiting for transfers between devices: 8.95 us -> none  [local(): weight = lax.all_gather(triple_rows, 'fy', axis=0, tiled=True)]
    all_gather x2, blocking collectives: 38.1 us -> 46.4 us  [the longest x1 24.2 us: local(): totals = lax.all_gather(total, 'dp', axis=0, tiled=True)]
    all_to_all x4 -> x3, blocking collectives: 79.9 us -> 87.6 us  [exchange(): return lax.all_to_all(x, axis, 0, 0, tiled=True)]
    all_to_all x1, starting transfers between devices: 8.55 us -> 12.9 us  [exchange(): return lax.all_to_all(x, axis, 0, 0, tiled=True)]
    unnamed x26 -> x23, local copies, waits for them, and re-layouts: 1.42 us -> 4.44 us
    ppermute x0 -> x1, waiting for transfers between devices: none -> 2.38 us  [local(): far = lax.ppermute(near, 'fx', [(i, i ^ 1) for i in range(GX)])]
    ppermute x0 -> x1, starting transfers between devices: none -> 2.04 us  [local(): far = lax.ppermute(near, 'fx', [(i, i ^ 1) for i in range(GX)])]
  transfers between devices with their start and end apart: 2 -> 2, of which waited for: 2 -> 1; matrix products, arithmetic and copies ran while one was open for 0% -> 1% of each run, Pallas kernels for 1% -> 1%
where the time goes in v2:
time: 174 us
  blocking collectives  134 us (77%)
  Pallas kernels  16.2 us (9%)
  starting transfers between devices  14.9 us (9%)
  local copies, waits for them, and re-layouts  4.69 us (3%)
  waiting for transfers between devices  2.38 us (1%)
    all_to_all x3, blocking collectives, exchange(): return lax.all_to_all(x, axis, 0, 0, tiled=True)  87.6 us
    all_gather x1, blocking collectives, local(): totals = lax.all_gather(total, 'dp', axis=0, tiled=True)  24.2 us
    all_gather x1, blocking collectives, local(): packed = lax.all_gather(packed[None], 'fx', axis=0, tiled=True)  22.2 us
    pallas_call x7, Pallas kernels, call(): pl.pallas_call(kernel, out_shape=shapes if many else shapes[0], in_specs=...  16.2 us
    all_to_all x1, starting transfers between devices, exchange(): return lax.all_to_all(x, axis, 0, 0, tiled=True)  12.9 us
    unnamed x23, local copies, waits for them, and re-layouts  4.44 us
  transfers between devices with their start and end apart: 2, of which 1 were waited for; matrix products, arithmetic and copies ran while one was open for 1% of the time, Pallas kernels for 1%

profile of v2, /device:TPU:2, one launch (start us, length us, event | category | flops | bytes accessed | tf_op | source)
XLA Modules:
  0.0 173.6 jit_solution(4098162754255898824)
XLA Ops:
  0.6 0.0 copy-start.9
  0.6 0.0 copy-start.8
  0.7 1.2 copy.15
  1.9 0.0 copy-start.1
  1.9 0.0 copy-start.3
  1.9 1.1 copy-done.3
  3.0 2.6 %spatial_context.1 = bf16[128,16,128]{2,1,0:T(8,128)(2,1)} custom-call(bf16[128,1728]{1,0:T(8,128)(2,1)S(1)} %bitcast.14, bf16[128,1152]{1,0:T(8,128)(2,1)S(1)} %bitcast.18), custom_call_target="tpu_custom_call" | custom-call | tf_op jit(solution)/shard_map/spatial_context/pallas_call | solution.py:229
  5.7 12.9 %all-to-all-start = ((bf16[128,16,128]{2,1,0:T(8,128)(2,1)}), bf16[128,16,128]{2,1,0:T(8,128)(2,1)S(1)}, u32[]{:S(2)}, u32[]{:S(2)}) async-start(bf16[128,16,128]{2,1,0:T(8,128)(2,1)} %spatial_context.1), calls=%async_computation | async-start | bytes 1048576 | tf_op jit(solution)/shard_map/all_to_all | solution.py:247
  18.6 0.0 copy-done.9
  18.6 0.1 fusion.1
  18.6 0.0 copy-done.8
  18.6 0.1 fusion
  18.7 0.1 concatenate.3
  18.8 22.2 %all-gather.1.packed = bf16[8,9,2304]{2,1,0:T(8,128)(2,1)S(1)} all-gather(bf16[1,9,2304]{2,1,0:T(8,128)(2,1)S(1)} %bitcast.19), channel_id=2, replica_groups=mesh['fx'=8,'fy'=16,'dp'=4] {'fx'}, dimensions={0}, use_global_device_ids=true | all-gather | bytes 373248 | tf_op jit(solution)/shard_map/all_gather | solution.py:261
  41.0 0.0 all-to-all-done.tokens
  41.0 0.0 copy-done.1
  41.0 0.3 forward.1
  41.3 0.0 copy-start.6
  41.3 40.9 %all_to_all.20 = bf16[16,72,1152]{2,1,0:T(8,128)(2,1)S(1)} all-to-all(bf16[16,72,1152]{2,1,0:T(8,128)(2,1)S(1)} %forward.1), channel_id=1, replica_groups=mesh['fx'=8,'fy'=16,'dp'=4] {'fy'}, dimensions={0} | all-to-all | bytes 5308416 | tf_op jit(solution)/shard_map/all_to_all | solution.py:247
  82.2 0.0 copy-start
  82.2 0.0 copy-start.4
  82.2 2.0 %collective-permute-start = (bf16[1152,1152]{1,0:T(8,128)(2,1)S(1)}, bf16[1152,1152]{1,0:T(8,128)(2,1)}, u32[]{:S(2)}, u32[]{:S(2)}) collective-permute-start(bf16[1152,1152]{1,0:T(8,128)(2,1)S(1)} %bitcast.11), channel_id=1, source_target_pairs={{0,64},{64,0},{128,192},{192,128},{256,320},{320,256},{384,448},{4... | collective-permute-start | bytes 7962632 | tf_op jit(solution)/shard_map/ppermute | solution.py:278
  84.3 1.1 copy.16
  85.4 0.0 copy-done.6
  85.4 1.6 hidden_near.1.placed
  87.0 2.4 %collective-permute-done.far = bf16[1152,1152]{1,0:T(8,128)(2,1)} collective-permute-done((bf16[1152,1152]{1,0:T(8,128)(2,1)S(1)}, bf16[1152,1152]{1,0:T(8,128)(2,1)}, u32[]{:S(2)}, u32[]{:S(2)}) %collective-permute-start) | collective-permute-done | bytes 2654240 | tf_op jit(solution)/shard_map/ppermute | solution.py:278
  89.3 0.0 copy-done
  89.3 0.0 copy-done.4
  89.4 8.4 %temporal_back.1 = (bf16[16,88,576]{2,1,0:T(8,128)(2,1)S(1)}, bf16[1152,576]{1,0:T(8,128)(2,1)S(1)}) custom-call(s32[1]{0:T(128)} %bitcast.core, bf16[1152,1152]{1,0:T(8,128)(2,1)} %bitcast.13, bf16[1152,1152]{1,0:T(8,128)(2,1)} %collective-permute-done.far, f32[128,1152]{1,0:T(8,128)S(1)} %hidden_near.1.placed, ...), custom_call_target="tpu_custom_call" | custom-call | tf_op jit(solution)/shard_map/temporal_back/pallas_call | solution.py:229
  97.8 0.0 copy-start.5
  97.8 0.0 copy-start.2
  97.8 0.0 copy-start.7
  97.8 28.7 %all_to_all.21.received = bf16[16,88,576]{2,1,0:T(8,128)(2,1)S(1)} all-to-all(bf16[16,88,576]{2,1,0:T(8,128)(2,1)S(1)} %get-tuple-element.11), channel_id=1, replica_groups=mesh['fx'=8,'fy'=16,'dp'=4] {'fy'}, dimensions={0} | all-to-all | bytes 3244032 | tf_op jit(solution)/shard_map/all_to_all | solution.py:247
  126.5 0.0 copy-done.5
  126.5 0.5 turn.1
  127.0 18.0 %all_to_all.22.received = bf16[8,24,1152]{2,1,0:T(8,128)(2,1)S(1)} all-to-all(bf16[8,24,1152]{2,1,0:T(8,128)(2,1)S(1)} %turn.1), channel_id=1, replica_groups=mesh['fx'=8,'fy'=16,'dp'=4] {'fx'}, dimensions={0} | all-to-all | bytes 884736 | tf_op jit(solution)/shard_map/all_to_all | solution.py:247
  145.0 0.0 copy-done.2
  145.0 0.0 copy-done.7
  145.0 2.6 %spatial_back.1 = (bf16[128,1728]{1,0:T(8,128)(2,1)S(1)}, bf16[128,1152]{1,0:T(8,128)(2,1)}) custom-call(bf16[8,24,1152]{2,1,0:T(8,128)(2,1)S(1)} %all_to_all.22.received, bf16[1152,576]{1,0:T(8,128)(2,1)S(1)} %get-tuple-element.12.out_rows, bf16[128,1728]{1,0:T(8,128)(2,1)S(1)} %bitcast.15, s32[1,1152]{1,0:T(1,128)S(1)} %copy-done.7), custom_call_target="tpu_custom_call" | custom-call | tf_op jit(solution)/shard_map/spatial_back/pallas_call | solution.py:229
  147.6 1.0 copy.17
  148.6 0.1 weight_sum.1
  148.7 24.2 %all_gather.7 = f32[4,9,576]{2,1,0:T(8,128)S(1)} all-gather(f32[1,9,576]{2,1,0:T(8,128)S(1)} %weight_sum.1), channel_id=1, replica_groups=mesh['fx'=8,'fy'=16,'dp'=4] {'dp'}, dimensions={0}, use_global_device_ids=true | all-gather | bytes 103680 | tf_op jit(solution)/shard_map/all_gather | solution.py:313
  173.0 0.6 multiply_bitcast_fusion
  (1 shorter events, 0.0 us)
Async XLA Ops:
  0.6 17.9 %copy-start.9 = (bf16[576,9]{0,1:T(8,128)(2,1)S(1)}, bf16[576,9]{0,1:T(8,128)(2,1)}, u32[]{:S(2)}) copy-start(bf16[576,9]{0,1:T(8,128)(2,1)} %param.12) | copy-start | bytes 31108
  0.6 18.0 %copy-start.8 = (bf16[9,1728]{1,0:T(8,128)(2,1)S(1)}, bf16[9,1728]{1,0:T(8,128)(2,1)}, u32[]{:S(2)}) copy-start(bf16[9,1728]{1,0:T(8,128)(2,1)} %param.13) | copy-start | bytes 93316
  1.9 39.1 %copy-start.1 = (bf16[1,1,128,1728]{3,2,1,0:T(8,128)(2,1)}, bf16[1,1,128,1728]{3,2,1,0:T(8,128)(2,1)S(1)}, u32[]{:S(2)}) copy-start(bf16[1,1,128,1728]{3,2,1,0:T(8,128)(2,1)S(1)} %copy.15) | copy-start | bytes 1327108
  1.9 1.1 copy-start.3
  5.7 35.3 %all-to-all-start = ((bf16[128,16,128]{2,1,0:T(8,128)(2,1)}), bf16[128,16,128]{2,1,0:T(8,128)(2,1)S(1)}, u32[]{:S(2)}, u32[]{:S(2)}) async-start(bf16[128,16,128]{2,1,0:T(8,128)(2,1)} %spatial_context.1), calls=%async_computation | async-start | bytes 1048576 | tf_op jit(solution)/shard_map/all_to_all | solution.py:247
  41.3 44.0 %copy-start.6 = (s32[1,1152]{1,0:T(1,128)S(1)}, s32[1,1152]{1,0:T(1,128)}, u32[]{:S(2)}) copy-start(s32[1,1152]{1,0:T(1,128)} %constant.32.clone.feature_at) | copy-start | bytes 13828
  82.2 7.1 %copy-start = (bf16[16,72,1152]{2,1,0:T(8,128)(2,1)}, bf16[16,72,1152]{2,1,0:T(8,128)(2,1)S(1)}, u32[]{:S(2)}) copy-start(bf16[16,72,1152]{2,1,0:T(8,128)(2,1)S(1)} %all_to_all.20) | copy-start | bytes 7962628
  82.2 7.1 %copy-start.4 = (s32[128,1]{1,0:T(8,128)S(1)}, s32[128,1]{1,0:T(8,128)}, u32[]{:S(2)}) copy-start(s32[128,1]{1,0:T(8,128)} %constant.33.clone.row_at) | copy-start | bytes 1540
  82.2 7.1 %collective-permute-start = (bf16[1152,1152]{1,0:T(8,128)(2,1)S(1)}, bf16[1152,1152]{1,0:T(8,128)(2,1)}, u32[]{:S(2)}, u32[]{:S(2)}) collective-permute-start(bf16[1152,1152]{1,0:T(8,128)(2,1)S(1)} %bitcast.11), channel_id=1, source_target_pairs={{0,64},{64,0},{128,192},{192,128},{256,320},{320,256},{384,448},{4... | collective-permute-start | bytes 7962632 | tf_op jit(solution)/shard_map/ppermute | solution.py:278
  97.8 28.8 %copy-start.5 = (s32[128,1]{1,0:T(8,128)S(1)}, s32[128,1]{1,0:T(8,128)}, u32[]{:S(2)}) copy-start(s32[128,1]{1,0:T(8,128)} %constant.34.clone.row_back) | copy-start | bytes 1540
  97.8 47.2 %copy-start.2 = (bf16[1,1,128,1728]{3,2,1,0:T(8,128)(2,1)S(1)}, bf16[1,1,128,1728]{3,2,1,0:T(8,128)(2,1)}, u32[]{:S(2)}) copy-start(bf16[1,1,128,1728]{3,2,1,0:T(8,128)(2,1)} %copy-done.1) | copy-start | bytes 1327108
  97.8 47.2 %copy-start.7 = (s32[1,1152]{1,0:T(1,128)S(1)}, s32[1,1152]{1,0:T(1,128)}, u32[]{:S(2)}) copy-start(s32[1,1152]{1,0:T(1,128)} %constant.35.clone.place_of) | copy-start | bytes 13828

commit v3 on v2

--- a/solution.py
+++ b/solution.py
@@ -26,9 +26,6 @@
 _j, _i, _r = _place // 72, (_place // 9) % 8, _place % 9
 FEATURE_AT = ((_i * GY + _j) * ROWS + _r).astype(np.int32)
 PLACE_OF = np.argsort(FEATURE_AT).astype(np.int32)
-_t = np.arange(TOKENS)
-ROW_AT = ((_t % 8) * 16 + _t // 8).astype(np.int32)
-ROW_BACK = ((_t % 16) * 8 + _t // 16).astype(np.int32)
 
 
 def dot(a, b, dims):
@@ -52,9 +49,12 @@
     return jnp.where(at == source, 1.0, 0.0).astype(BF)
 
 
-def pick_rows(source, columns):
-    at = lax.broadcasted_iota(jnp.int32, (source.shape[0], columns), 1)
-    return jnp.where(at == source, 1.0, 0.0).astype(BF)
+def turn_rows(minor):
+    row = lax.broadcasted_iota(jnp.int32, (TOKENS, TOKENS), 0)
+    column = lax.broadcasted_iota(jnp.int32, (TOKENS, TOKENS), 1)
+    shift = minor.bit_length() - 1
+    source = (row & (minor - 1)) * (TOKENS // minor) + (row >> shift)
+    return jnp.where(column == source, 1.0, 0.0).astype(BF)
 
 
 def stack_heads(x):
@@ -77,16 +77,34 @@
     return e / jnp.sum(e, axis=-1, keepdims=True)
 
 
-def attend(q, k, v):
-    scores = nt(q, stack_heads(k))
+def stack_heads_turned(x):
+    row = lax.broadcasted_iota(jnp.int32, (INNER, 1), 0)
+    parts = []
+    for h in range(HEADS):
+        mask = jnp.where((row >= h * SIZE) & (row < (h + 1) * SIZE), 1.0, 0.0).astype(BF)
+        parts.append(x * mask)
+    return jnp.concatenate(parts, axis=1)
+
+
+def attend_turned(q, k, v):
+    scores = tn(q, stack_heads_turned(k))
     weights = [softmax(head_of(scores, h)).astype(BF) for h in range(HEADS)]
-    return nn(jnp.concatenate(weights, axis=1), stack_heads(v))
-
-
-def attend_back(q, k, v, cot):
-    stacked_k = stack_heads(k)
-    scores = nt(q, stacked_k)
-    grad_weights = nt(cot, stack_heads(v))
+    return nt(jnp.concatenate(weights, axis=1), stack_heads_turned(v))
+
+
+def attend_back_turned(q, k, v, cot):
+    stacked_k = stack_heads_turned(k)
+    scores = tn(q, stacked_k)
+    grad_weights = nn(cot.astype(BF), stack_heads_turned(v))
+    weights, grad_scores = softmax_back(scores, grad_weights)
+    grad_q = nt(stacked_k, jnp.concatenate(grad_scores, axis=1))
+    grad_k = nn(stack_heads_turned(q), jnp.concatenate(grad_scores, axis=0))
+    cot_turned = jnp.transpose(cot).astype(BF)
+    grad_v = nn(stack_heads_turned(cot_turned), jnp.concatenate(weights, axis=0))
+    return grad_q, grad_k, grad_v
+
+
+def softmax_back(scores, grad_weights):
     weights, grad_scores = [], []
     for h in range(HEADS):
         p = softmax(head_of(scores, h))
@@ -94,6 +112,14 @@
         mean = jnp.sum(p * g, axis=-1, keepdims=True)
         weights.append(p.astype(BF))
         grad_scores.append((p * (g - mean) * SCALE).astype(BF))
+    return weights, grad_scores
+
+
+def attend_back(q, k, v, cot):
+    stacked_k = stack_heads(k)
+    scores = nt(q, stacked_k)
+    grad_weights = nt(cot, stack_heads(v))
+    weights, grad_scores = softmax_back(scores, grad_weights)
     grad_q = nn(jnp.concatenate(grad_scores, axis=1), stacked_k)
     grad_k = tn(jnp.concatenate(grad_scores, axis=0), stack_heads(q))
     grad_v = tn(jnp.concatenate(weights, axis=0), stack_heads(cot))
@@ -113,10 +139,14 @@
     return jnp.concatenate([held[:, t, :] for t in range(first, first + count)], axis=1)
 
 
-def context_kernel(triple, hidden_in, tokens, held):
-    q, k, v = split_triple(triple[...])
-    context = attend(q, k, v)
+def context_kernel(triple, hidden_there, tokens, held, hidden_in, arrived):
+    fetch = pltpu.make_async_copy(hidden_there, hidden_in, arrived)
+    fetch.start()
+    context = attend_turned(
+        triple[:INNER, :], triple[INNER:2 * INNER, :], triple[2 * INNER:, :]
+    )
     blank = jnp.zeros((TOKENS, 16 * 128 - D - INNER), F32)
+    fetch.wait()
     spread(jnp.concatenate([hidden_in[...].astype(F32), context, blank], axis=1), held)
     tokens[...] = held[...].astype(BF)
 
@@ -129,16 +159,18 @@
         copies[j] = part
 
 
-def place_kernel(core, near, tokens, feature_at, placed, held):
+def place_kernel(core, near, tokens, feature_at, placed, near_copy, held):
     held[...] = tokens[...].astype(F32)
     hidden_in = collect(held, 0, 9).astype(BF)
     ctx32 = collect(held, 9, 5)[:, :INNER]
     half = jnp.where(core[0] == 0, ctx32[:, :REST], ctx32[:, REST:]).astype(BF)
-    placed[...] = nn(hidden_in, pick_columns(D, feature_at[...])) + nt(half, near[:, PART:])
+    near_copy[...] = near[...]
+    mixed = jnp.transpose(nt(near[:, PART:], half))
+    placed[...] = nn(hidden_in, pick_columns(D, feature_at[...])) + mixed
 
 
 def temporal_kernel(
-    core, near, far, placed, tokens, cotangent, row_at, message, out_rows, held
+    core, near, far, placed, tokens, cotangent, message, out_rows, held
 ):
     first = core[0] == 0
     w_near = near[...]
@@ -151,7 +183,7 @@
     ctx32 = collect(held, 1, 5)[:, :INNER]
     half = jnp.where(first, ctx32[:, REST:], ctx32[:, :REST]).astype(BF)
 
-    hidden = (placed[...] + nt(half, far_out)).astype(BF).astype(F32)
+    hidden = (placed[...] + jnp.transpose(nt(far_out, half))).astype(BF).astype(F32)
     centred = hidden - jnp.mean(hidden, axis=-1, keepdims=True)
     scale = lax.rsqrt(jnp.mean(centred * centred, axis=-1, keepdims=True) + 1e-06)
     normal = centred * scale
@@ -166,13 +198,14 @@
     blank = jnp.zeros((TOKENS, REST), F32)
     left = jnp.concatenate([grads[:, :PART], blank], axis=1)
     right = jnp.concatenate([grads[:, PART:], blank], axis=1)
-    grad_normal = nt(jnp.where(first, left, right).astype(BF), w_near) + nt(
-        jnp.where(first, right, left).astype(BF), w_far
+    grad_normal = jnp.transpose(
+        nt(w_near, jnp.where(first, left, right).astype(BF))
+        + nt(w_far, jnp.where(first, right, left).astype(BF))
     )
     along = jnp.mean(grad_normal * normal, axis=-1, keepdims=True)
     level = jnp.mean(grad_normal, axis=-1, keepdims=True)
     grad_hidden = (scale * (grad_normal - level - normal * along)).astype(BF)
-    turned = nn(pick_rows(row_at[...], TOKENS), grad_hidden)
+    turned = nn(turn_rows(GX), grad_hidden)
     low, high = turned[:, :INNER], turned[:, INNER:]
     term = tn(grad_hidden, ctx32.astype(BF))
     for j in range(GY):
@@ -186,7 +219,7 @@
         ).astype(BF)
 
 
-def turn_kernel(received, row_back, message, held):
+def turn_kernel(received, message, held):
     one = received[0].astype(F32)
     total, low, high = one[16:], [one[:8]], [one[8:16]]
     for j in range(1, GY):
@@ -196,7 +229,7 @@
         high.append(one[8:16])
     held[:72, :] = total
     held[72:, :] = jnp.zeros((8, INNER), F32)
-    turn = pick_rows(row_back[...], TOKENS)
+    turn = turn_rows(GY)
     low = nn(turn, jnp.concatenate(low, axis=0).astype(BF)).astype(BF)
     high = nn(turn, jnp.concatenate(high, axis=0).astype(BF)).astype(BF)
     for i in range(GX):
@@ -218,19 +251,27 @@
 def final_kernel(received, out_rows, triple, place_of, grad_triple, grad_hidden):
     grad = received[:, :16, :].reshape(TOKENS, D)
     grad_hidden[...] = nn(grad, pick_columns(D, place_of[...])).astype(BF)
-    cot = nn(grad, out_rows[...]).astype(BF)
-    q, k, v = split_triple(triple[...])
-    grad_triple[...] = jnp.concatenate(attend_back(q, k, v, cot), axis=1).astype(BF)
-
-
-def call(kernel, name, outs, *args, scratch=()):
+    grads = attend_back_turned(
+        triple[:INNER, :],
+        triple[INNER:2 * INNER, :],
+        triple[2 * INNER:, :],
+        nn(grad, out_rows[...]),
+    )
+    for n, part in enumerate(grads):
+        grad_triple[n * INNER:(n + 1) * INNER, :] = part.astype(BF)
+
+
+def call(kernel, name, outs, *args, scratch=(), there=()):
     many = isinstance(outs, list)
     shapes = [jax.ShapeDtypeStruct(s, t) for s, t in (outs if many else [outs])]
     return pl.pallas_call(
         kernel,
         out_shape=shapes if many else shapes[0],
         in_specs=[
-            pl.BlockSpec(memory_space=pltpu.SMEM if a.ndim == 1 else pltpu.VMEM) for a in args
+            pl.BlockSpec(
+                memory_space=pl.ANY if n in there else pltpu.SMEM if a.ndim == 1 else pltpu.VMEM
+            )
+            for n, a in enumerate(args)
         ],
         out_specs=(
             [pl.BlockSpec(memory_space=pltpu.VMEM)] * len(shapes)
@@ -249,7 +290,7 @@
 
 def local(hidden_in, spatial_triple, context_grad, out_weight, triple_weight):
     hidden_in = hidden_in.reshape(TOKENS, D)
-    spatial = spatial_triple.reshape(TOKENS, 3 * INNER)
+    spatial = spatial_triple.reshape(TOKENS, 3 * INNER).T
     cotangent = context_grad.reshape(TOKENS, INNER)
 
     core = (lax.axis_index("fx") % 2).astype(jnp.int32)[None]
@@ -262,7 +303,13 @@
     slabs = (TOKENS, 16, 128)
     held = pltpu.VMEM(slabs, F32)
     tokens = call(
-        context_kernel, "spatial_context", (slabs, BF), spatial, hidden_in, scratch=[held]
+        context_kernel,
+        "spatial_context",
+        (slabs, BF),
+        spatial,
+        hidden_in,
+        scratch=[held, pltpu.VMEM((TOKENS, D), BF), pltpu.SemaphoreType.DMA],
+        there=(1,),
     )
     tokens = exchange(tokens, ("fx", "fy"))
     packed, tokens = lax.optimization_barrier((packed, tokens))
@@ -276,10 +323,10 @@
     )
     near = exchange(near, "fy").reshape(D, D)
     far = lax.ppermute(near, "fx", [(i, i ^ 1) for i in range(GX)])
-    placed = call(
+    placed, near = call(
         place_kernel,
         "hidden_near",
-        ((TOKENS, D), F32),
+        [((TOKENS, D), F32), ((D, D), BF)],
         core,
         near,
         tokens,
@@ -296,7 +343,6 @@
         placed,
         tokens,
         cotangent,
-        ROW_AT[:, None],
         scratch=[pltpu.VMEM((TOKENS, 8, 128), F32)],
     )
     message = exchange(message, "fy")
@@ -305,7 +351,6 @@
         "turn",
         ((GX, 24, D), BF),
         message,
-        ROW_BACK[:, None],
         scratch=[pltpu.VMEM((80, INNER), F32)],
     )
     message = exchange(message, "fx")
@@ -314,7 +359,7 @@
     grad_triple, grad_hidden = call(
         final_kernel,
         "spatial_back",
-        [((TOKENS, 3 * INNER), BF), ((TOKENS, D), BF)],
+        [((3 * INNER, TOKENS), BF), ((TOKENS, D), BF)],
         message,
         out_rows,
         spatial,
@@ -322,7 +367,7 @@
     )
     grad_out_weight = (jnp.sum(totals, axis=0) / CLIP_GROUPS).T
     return (
-        grad_triple.reshape(1, 1, TOKENS, 3 * INNER),
+        grad_triple.T.reshape(1, 1, TOKENS, 3 * INNER),
         grad_hidden.reshape(1, 1, TOKENS, D),
         grad_out_weight,
     )

time: 174 us -> 174 us (level)
  Pallas kernels: 16.2 us -> 18.6 us
  waiting for transfers between devices: 2.38 us -> 0.04 us
    pallas_call x7, Pallas kernels: 16.2 us -> 18.6 us  [call(): pl.pallas_call(kernel, out_shape=shapes if many else shapes[0], in_specs=...]
    ppermute x1, waiting for transfers between devices: 2.38 us -> 0.04 us  [local(): far = lax.ppermute(near, 'fx', [(i, i ^ 1) for i in range(GX)])]
    unnamed x23 -> x17, local copies, waits for them, and re-layouts: 4.44 us -> 3.67 us
  transfers between devices with their start and end apart: 2 -> 2, of which waited for: 1 -> 0; matrix products, arithmetic and copies ran while one was open for 1% -> 1% of each run, Pallas kernels for 1% -> 2%
where the time goes in v3:
time: 174 us; the launch traced here: 173 us
  blocking collectives  133 us (76%)
  Pallas kernels  18.6 us (11%)
  starting transfers between devices  14.8 us (9%)
  local copies, waits for them, and re-layouts  5.53 us (3%)
    all_to_all x3, blocking collectives, exchange(): return lax.all_to_all(x, axis, 0, 0, tiled=True)  88 us
    all_gather x1, blocking collectives, local(): totals = lax.all_gather(total, 'dp', axis=0, tiled=True)  24.2 us
    all_gather x1, blocking collectives, local(): packed = lax.all_gather(packed[None], 'fx', axis=0, tiled=True)  20.6 us
    pallas_call x7, Pallas kernels, call(): pl.pallas_call(kernel, out_shape=shapes if many else shapes[0], in_specs=...  18.6 us
    all_to_all x1, starting transfers between devices, exchange(): return lax.all_to_all(x, axis, 0, 0, tiled=True)  12.9 us
    unnamed x17, local copies, waits for them, and re-layouts  3.67 us
  transfers between devices with their start and end apart: 2, of which 0 were waited for; matrix products, arithmetic and copies ran while one was open for 1% of the time, Pallas kernels for 2%

profile of v3, /device:TPU:2, one launch (start us, length us, event | category | flops | bytes accessed | tf_op | source)
XLA Modules:
  0.0 173.2 jit_solution(15983949584027158920)
XLA Ops:
  0.6 0.0 copy-start.1
  0.6 1.0 copy-done.1
  1.6 0.0 copy-start.3
  1.6 1.0 copy-done.3
  2.6 2.6 %spatial_context.1 = bf16[128,16,128]{2,1,0:T(8,128)(2,1)} custom-call(bf16[1728,128]{1,0:T(8,128)(2,1)S(1)} %bitcast.15, bf16[128,1152]{1,0:T(8,128)(2,1)S(1)} %bitcast.18), custom_call_target="tpu_custom_call" | custom-call | tf_op jit(solution)/shard_map/spatial_context/pallas_call | solution.py:267
  5.2 12.9 %all-to-all-start = ((bf16[128,16,128]{2,1,0:T(8,128)(2,1)}), bf16[128,16,128]{2,1,0:T(8,128)(2,1)S(1)}, u32[]{:S(2)}, u32[]{:S(2)}) async-start(bf16[128,16,128]{2,1,0:T(8,128)(2,1)} %spatial_context.1), calls=%async_computation | async-start | bytes 1048576 | tf_op jit(solution)/shard_map/all_to_all | solution.py:288
  18.1 0.9 fusion.1
  19.0 0.9 fusion
  19.9 0.1 concatenate.3
  20.0 20.6 %all-gather.1.packed = bf16[8,9,2304]{2,1,0:T(8,128)(2,1)S(1)} all-gather(bf16[1,9,2304]{2,1,0:T(8,128)(2,1)S(1)} %bitcast.21), channel_id=2, replica_groups=mesh['fx'=8,'fy'=16,'dp'=4] {'fx'}, dimensions={0}, use_global_device_ids=true | all-gather | bytes 373248 | tf_op jit(solution)/shard_map/all_gather | solution.py:302
  40.5 0.0 all-to-all-done.tokens
  40.6 0.3 forward.1
  40.9 0.0 copy-start.7
  40.9 0.0 copy-start.4
  40.9 41.0 %all_to_all.20 = bf16[16,72,1152]{2,1,0:T(8,128)(2,1)S(1)} all-to-all(bf16[16,72,1152]{2,1,0:T(8,128)(2,1)S(1)} %forward.1), channel_id=1, replica_groups=mesh['fx'=8,'fy'=16,'dp'=4] {'fy'}, dimensions={0} | all-to-all | bytes 5308416 | tf_op jit(solution)/shard_map/all_to_all | solution.py:288
  81.9 0.0 copy-start.6
  81.9 1.9 %collective-permute-start = (bf16[1152,1152]{1,0:T(8,128)(2,1)S(1)}, bf16[1152,1152]{1,0:T(8,128)(2,1)}, u32[]{:S(2)}, u32[]{:S(2)}) collective-permute-start(bf16[1152,1152]{1,0:T(8,128)(2,1)S(1)} %bitcast.19), channel_id=1, source_target_pairs={{0,64},{64,0},{128,192},{192,128},{256,320},{320,256},{384,448},{4... | collective-permute-start | bytes 7962632 | tf_op jit(solution)/shard_map/ppermute | solution.py:325
  83.8 0.0 copy-done.7
  83.9 0.2 copy.11
  84.0 0.0 copy-done.6
  84.0 0.0 copy-done.4
  84.0 3.3 %hidden_near.1 = (f32[128,1152]{1,0:T(8,128)S(1)}, bf16[1152,1152]{1,0:T(8,128)(2,1)S(1)}) custom-call(s32[1]{0:T(128)} %bitcast.core, bf16[1152,1152]{1,0:T(8,128)(2,1)} %bitcast.20, bf16[128,16,128]{2,1,0:T(8,128)(2,1)S(1)} %all-to-all-done.tokens, s32[1,1152]{1,0:T(1,128)S(1)} %copy-done.4), custom_call_target="tpu_custom_call" | custom-call | tf_op jit(solution)/shard_map/hidden_near/pallas_call | solution.py:267
  87.3 0.0 copy-start
  87.3 1.5 copy-done
  88.9 0.0 collective-permute-done.far
  88.9 8.6 %temporal_back.1 = (bf16[16,88,576]{2,1,0:T(8,128)(2,1)S(1)}, bf16[1152,576]{1,0:T(8,128)(2,1)S(1)}) custom-call(s32[1]{0:T(128)} %bitcast.core, bf16[1152,1152]{1,0:T(8,128)(2,1)} %copy-done, bf16[1152,1152]{1,0:T(8,128)(2,1)} %collective-permute-done.far, f32[128,1152]{1,0:T(8,128)S(1)} %get-tuple-element.14.placed, ...), custom_call_target="tpu_custom_call" | custom-call | tf_op jit(solution)/shard_map/temporal_back/pallas_call | solution.py:267
  97.5 29.0 %all_to_all.21.received = bf16[16,88,576]{2,1,0:T(8,128)(2,1)S(1)} all-to-all(bf16[16,88,576]{2,1,0:T(8,128)(2,1)S(1)} %get-tuple-element.15), channel_id=1, replica_groups=mesh['fx'=8,'fy'=16,'dp'=4] {'fy'}, dimensions={0} | all-to-all | bytes 3244032 | tf_op jit(solution)/shard_map/all_to_all | solution.py:288
  126.5 0.0 copy-start.2
  126.5 0.0 copy-start.5
  126.5 0.5 turn.1
  127.0 18.0 %all_to_all.22.received = bf16[8,24,1152]{2,1,0:T(8,128)(2,1)S(1)} all-to-all(bf16[8,24,1152]{2,1,0:T(8,128)(2,1)S(1)} %turn.1), channel_id=1, replica_groups=mesh['fx'=8,'fy'=16,'dp'=4] {'fx'}, dimensions={0} | all-to-all | bytes 884736 | tf_op jit(solution)/shard_map/all_to_all | solution.py:288
  144.9 0.1 weight_sum.1
  145.0 24.2 %all_gather.7 = f32[4,9,576]{2,1,0:T(8,128)S(1)} all-gather(f32[1,9,576]{2,1,0:T(8,128)S(1)} %weight_sum.1), channel_id=1, replica_groups=mesh['fx'=8,'fy'=16,'dp'=4] {'dp'}, dimensions={0}, use_global_device_ids=true | all-gather | bytes 103680 | tf_op jit(solution)/shard_map/all_gather | solution.py:358
  169.3 0.6 multiply_bitcast_fusion
  169.9 0.0 copy-done.2
  169.9 0.0 copy-done.5
  169.9 3.3 %spatial_back.1 = (bf16[1728,128]{1,0:T(8,128)(2,1)}, bf16[128,1152]{1,0:T(8,128)(2,1)}) custom-call(bf16[8,24,1152]{2,1,0:T(8,128)(2,1)S(1)} %all_to_all.22.received, bf16[1152,576]{1,0:T(8,128)(2,1)S(1)} %get-tuple-element.16.out_rows, bf16[1728,128]{1,0:T(8,128)(2,1)S(1)} %bitcast.16, s32[1,1152]{1,0:T(1,128)S(1)} %copy-done.5), custom_call_target="tpu_custom_call" | custom-call | tf_op jit(solution)/shard_map/spatial_back/pallas_call | solution.py:267
  (1 shorter events, 0.0 us)
Async XLA Ops:
  0.6 1.0 copy-start.1
  1.6 1.0 copy-start.3
  5.2 35.4 %all-to-all-start = ((bf16[128,16,128]{2,1,0:T(8,128)(2,1)}), bf16[128,16,128]{2,1,0:T(8,128)(2,1)S(1)}, u32[]{:S(2)}, u32[]{:S(2)}) async-start(bf16[128,16,128]{2,1,0:T(8,128)(2,1)} %spatial_context.1), calls=%async_computation | async-start | bytes 1048576 | tf_op jit(solution)/shard_map/all_to_all | solution.py:288
  40.9 43.0 %copy-start.7 = (bf16[1,128,1,576]{1,3,2,0:T(8,128)(2,1)S(1)}, bf16[1,128,1,576]{1,3,2,0:T(8,128)(2,1)}, u32[]{:S(2)}) copy-start(bf16[1,128,1,576]{1,3,2,0:T(8,128)(2,1)} %param.9) | copy-start | bytes 442372
  40.9 43.1 %copy-start.4 = (s32[1,1152]{1,0:T(1,128)S(1)}, s32[1,1152]{1,0:T(1,128)}, u32[]{:S(2)}) copy-start(s32[1,1152]{1,0:T(1,128)} %constant.28.clone.feature_at) | copy-start | bytes 13828
  81.9 2.1 %copy-start.6 = (bf16[16,72,1152]{2,1,0:T(8,128)(2,1)}, bf16[16,72,1152]{2,1,0:T(8,128)(2,1)S(1)}, u32[]{:S(2)}) copy-start(bf16[16,72,1152]{2,1,0:T(8,128)(2,1)S(1)} %all_to_all.20) | copy-start | bytes 7962628
  81.9 7.0 %collective-permute-start = (bf16[1152,1152]{1,0:T(8,128)(2,1)S(1)}, bf16[1152,1152]{1,0:T(8,128)(2,1)}, u32[]{:S(2)}, u32[]{:S(2)}) collective-permute-start(bf16[1152,1152]{1,0:T(8,128)(2,1)S(1)} %bitcast.19), channel_id=1, source_target_pairs={{0,64},{64,0},{128,192},{192,128},{256,320},{320,256},{384,448},{4... | collective-permute-start | bytes 7962632 | tf_op jit(solution)/shard_map/ppermute | solution.py:325
  87.3 1.5 copy-start
  126.5 43.4 %copy-start.2 = (bf16[1,1,128,1728]{2,3,1,0:T(8,128)(2,1)S(1)}, bf16[1,1,128,1728]{2,3,1,0:T(8,128)(2,1)}, u32[]{:S(2)}) copy-start(bf16[1,1,128,1728]{2,3,1,0:T(8,128)(2,1)} %param.8) | copy-start | bytes 1327108
  126.5 43.4 %copy-start.5 = (s32[1,1152]{1,0:T(1,128)S(1)}, s32[1,1152]{1,0:T(1,128)}, u32[]{:S(2)}) copy-start(s32[1,1152]{1,0:T(1,128)} %constant.29.clone.place_of) | copy-start | bytes 13828

commit v4 on v3

--- a/solution.py
+++ b/solution.py
@@ -139,14 +139,11 @@
     return jnp.concatenate([held[:, t, :] for t in range(first, first + count)], axis=1)
 
 
-def context_kernel(triple, hidden_there, tokens, held, hidden_in, arrived):
-    fetch = pltpu.make_async_copy(hidden_there, hidden_in, arrived)
-    fetch.start()
+def context_kernel(triple, hidden_in, tokens, held):
     context = attend_turned(
         triple[:INNER, :], triple[INNER:2 * INNER, :], triple[2 * INNER:, :]
     )
     blank = jnp.zeros((TOKENS, 16 * 128 - D - INNER), F32)
-    fetch.wait()
     spread(jnp.concatenate([hidden_in[...].astype(F32), context, blank], axis=1), held)
     tokens[...] = held[...].astype(BF)
 
@@ -159,12 +156,11 @@
         copies[j] = part
 
 
-def place_kernel(core, near, tokens, feature_at, placed, near_copy, held):
+def place_kernel(core, near, tokens, feature_at, placed, held):
     held[...] = tokens[...].astype(F32)
     hidden_in = collect(held, 0, 9).astype(BF)
     ctx32 = collect(held, 9, 5)[:, :INNER]
     half = jnp.where(core[0] == 0, ctx32[:, :REST], ctx32[:, REST:]).astype(BF)
-    near_copy[...] = near[...]
     mixed = jnp.transpose(nt(near[:, PART:], half))
     placed[...] = nn(hidden_in, pick_columns(D, feature_at[...])) + mixed
 
@@ -261,17 +257,14 @@
         grad_triple[n * INNER:(n + 1) * INNER, :] = part.astype(BF)
 
 
-def call(kernel, name, outs, *args, scratch=(), there=()):
+def call(kernel, name, outs, *args, scratch=()):
     many = isinstance(outs, list)
     shapes = [jax.ShapeDtypeStruct(s, t) for s, t in (outs if many else [outs])]
     return pl.pallas_call(
         kernel,
         out_shape=shapes if many else shapes[0],
         in_specs=[
-            pl.BlockSpec(
-                memory_space=pl.ANY if n in there else pltpu.SMEM if a.ndim == 1 else pltpu.VMEM
-            )
-            for n, a in enumerate(args)
+            pl.BlockSpec(memory_space=pltpu.SMEM if a.ndim == 1 else pltpu.VMEM) for a in args
         ],
         out_specs=(
             [pl.BlockSpec(memory_space=pltpu.VMEM)] * len(shapes)
@@ -308,8 +301,7 @@
         (slabs, BF),
         spatial,
         hidden_in,
-        scratch=[held, pltpu.VMEM((TOKENS, D), BF), pltpu.SemaphoreType.DMA],
-        there=(1,),
+        scratch=[held],
     )
     tokens = exchange(tokens, ("fx", "fy"))
     packed, tokens = lax.optimization_barrier((packed, tokens))
@@ -323,10 +315,10 @@
     )
     near = exchange(near, "fy").reshape(D, D)
     far = lax.ppermute(near, "fx", [(i, i ^ 1) for i in range(GX)])
-    placed, near = call(
+    placed = call(
         place_kernel,
         "hidden_near",
-        [((TOKENS, D), F32), ((D, D), BF)],
+        ((TOKENS, D), F32),
         core,
         near,
         tokens,

time: 174 us -> 174 us (level)
  waiting for transfers between devices: 0.04 us -> 3.52 us
  Pallas kernels: 18.6 us -> 16.3 us
    ppermute x1, waiting for transfers between devices: 0.04 us -> 3.51 us  [local(): far = lax.ppermute(near, 'fx', [(i, i ^ 1) for i in range(GX)])]
    pallas_call x7, Pallas kernels: 18.6 us -> 16.3 us  [call(): pl.pallas_call(kernel, out_shape=shapes if many else shapes[0], in_specs=...]
    unnamed x17 -> x19, local copies, waits for them, and re-layouts: 3.67 us -> 3.27 us
  transfers between devices with their start and end apart: 2 -> 2, of which waited for: 0 -> 1; matrix products, arithmetic and copies ran while one was open for 1% -> 1% of each run, Pallas kernels for 2% -> 1%
where the time goes in v4:
time: 174 us
  blocking collectives  133 us (76%)
  Pallas kernels  16.3 us (9%)
  starting transfers between devices  14.8 us (9%)
  local copies, waits for them, and re-layouts  5.13 us (3%)
  waiting for transfers between devices  3.52 us (2%)
    all_to_all x3, blocking collectives, exchange(): return lax.all_to_all(x, axis, 0, 0, tiled=True)  87.7 us
    all_gather x1, blocking collectives, local(): totals = lax.all_gather(total, 'dp', axis=0, tiled=True)  24.2 us
    all_gather x1, blocking collectives, local(): packed = lax.all_gather(packed[None], 'fx', axis=0, tiled=True)  20.6 us
    pallas_call x7, Pallas kernels, call(): pl.pallas_call(kernel, out_shape=shapes if many else shapes[0], in_specs=...  16.3 us
    all_to_all x1, starting transfers between devices, exchange(): return lax.all_to_all(x, axis, 0, 0, tiled=True)  12.9 us
    ppermute x1, waiting for transfers between devices, local(): far = lax.ppermute(near, 'fx', [(i, i ^ 1) for i in range(GX)])  3.51 us
  transfers between devices with their start and end apart: 2, of which 1 were waited for; matrix products, arithmetic and copies ran while one was open for 1% of the time, Pallas kernels for 1%

profile of v4, /device:TPU:2, one launch (start us, length us, event | category | flops | bytes accessed | tf_op | source)
XLA Modules:
  0.0 173.7 jit_solution(14417941532715755907)
XLA Ops:
  0.6 0.0 copy-start.1
  0.6 1.0 copy-done.1
  1.6 0.0 copy-start.5
  1.6 1.0 copy-done.5
  2.6 2.2 %spatial_context.1 = bf16[128,16,128]{2,1,0:T(8,128)(2,1)} custom-call(bf16[1728,128]{1,0:T(8,128)(2,1)S(1)} %bitcast.18, bf16[128,1152]{1,0:T(8,128)(2,1)S(1)} %bitcast.21), custom_call_target="tpu_custom_call" | custom-call | tf_op jit(solution)/shard_map/spatial_context/pallas_call | solution.py:263
  4.8 12.9 %all-to-all-start = ((bf16[128,16,128]{2,1,0:T(8,128)(2,1)}), bf16[128,16,128]{2,1,0:T(8,128)(2,1)S(1)}, u32[]{:S(2)}, u32[]{:S(2)}) async-start(bf16[128,16,128]{2,1,0:T(8,128)(2,1)} %spatial_context.1), calls=%async_computation | async-start | bytes 1048576 | tf_op jit(solution)/shard_map/all_to_all | solution.py:281
  17.7 0.9 fusion.1
  18.6 0.9 fusion
  19.5 0.1 concatenate.3
  19.6 20.6 %all-gather.1.packed = bf16[8,9,2304]{2,1,0:T(8,128)(2,1)S(1)} all-gather(bf16[1,9,2304]{2,1,0:T(8,128)(2,1)S(1)} %bitcast.22), channel_id=2, replica_groups=mesh['fx'=8,'fy'=16,'dp'=4] {'fx'}, dimensions={0}, use_global_device_ids=true | all-gather | bytes 373248 | tf_op jit(solution)/shard_map/all_gather | solution.py:295
  40.2 0.0 all-to-all-done.tokens
  40.2 0.3 forward.1
  40.5 0.0 copy-start.8
  40.5 0.0 copy-start.6
  40.5 41.0 %all_to_all.20 = bf16[16,72,1152]{2,1,0:T(8,128)(2,1)S(1)} all-to-all(bf16[16,72,1152]{2,1,0:T(8,128)(2,1)S(1)} %forward.1), channel_id=1, replica_groups=mesh['fx'=8,'fy'=16,'dp'=4] {'fy'}, dimensions={0} | all-to-all | bytes 5308416 | tf_op jit(solution)/shard_map/all_to_all | solution.py:281
  81.6 0.0 copy-start
  81.6 1.9 %collective-permute-start = (bf16[1152,1152]{1,0:T(8,128)(2,1)S(1)}, bf16[1152,1152]{1,0:T(8,128)(2,1)}, u32[]{:S(2)}, u32[]{:S(2)}) collective-permute-start(bf16[1152,1152]{1,0:T(8,128)(2,1)S(1)} %bitcast.15), channel_id=1, source_target_pairs={{0,64},{64,0},{128,192},{192,128},{256,320},{320,256},{384,448},{4... | collective-permute-start | bytes 7962632 | tf_op jit(solution)/shard_map/ppermute | solution.py:317
  83.5 0.0 copy-done.8
  83.5 0.2 copy.11
  83.6 0.0 copy-done.6
  83.7 1.3 hidden_near.1.placed
  85.0 3.5 %collective-permute-done.far = bf16[1152,1152]{1,0:T(8,128)(2,1)} collective-permute-done((bf16[1152,1152]{1,0:T(8,128)(2,1)S(1)}, bf16[1152,1152]{1,0:T(8,128)(2,1)}, u32[]{:S(2)}, u32[]{:S(2)}) %collective-permute-start) | collective-permute-done | bytes 2654240 | tf_op jit(solution)/shard_map/ppermute | solution.py:317
  88.5 0.0 copy-done
  88.5 8.6 %temporal_back.1 = (bf16[16,88,576]{2,1,0:T(8,128)(2,1)S(1)}, bf16[1152,576]{1,0:T(8,128)(2,1)S(1)}) custom-call(s32[1]{0:T(128)} %bitcast.core, bf16[1152,1152]{1,0:T(8,128)(2,1)} %bitcast.17, bf16[1152,1152]{1,0:T(8,128)(2,1)} %collective-permute-done.far, f32[128,1152]{1,0:T(8,128)S(1)} %hidden_near.1.placed, ...), custom_call_target="tpu_custom_call" | custom-call | tf_op jit(solution)/shard_map/temporal_back/pallas_call | solution.py:263
  97.2 0.0 copy-start.3
  97.2 1.1 copy-done.3
  98.3 28.6 %all_to_all.21.received = bf16[16,88,576]{2,1,0:T(8,128)(2,1)S(1)} all-to-all(bf16[16,88,576]{2,1,0:T(8,128)(2,1)S(1)} %get-tuple-element.11), channel_id=1, replica_groups=mesh['fx'=8,'fy'=16,'dp'=4] {'fy'}, dimensions={0} | all-to-all | bytes 3244032 | tf_op jit(solution)/shard_map/all_to_all | solution.py:281
  126.9 0.0 copy-start.2
  126.9 0.0 copy-start.4
  126.9 0.0 copy-start.7
  126.9 0.5 turn.1
  127.3 18.1 %all_to_all.22.received = bf16[8,24,1152]{2,1,0:T(8,128)(2,1)S(1)} all-to-all(bf16[8,24,1152]{2,1,0:T(8,128)(2,1)S(1)} %turn.1), channel_id=1, replica_groups=mesh['fx'=8,'fy'=16,'dp'=4] {'fx'}, dimensions={0} | all-to-all | bytes 884736 | tf_op jit(solution)/shard_map/all_to_all | solution.py:281
  145.4 0.1 weight_sum.1
  145.5 24.2 %all_gather.7 = f32[4,9,576]{2,1,0:T(8,128)S(1)} all-gather(f32[1,9,576]{2,1,0:T(8,128)S(1)} %weight_sum.1), channel_id=1, replica_groups=mesh['fx'=8,'fy'=16,'dp'=4] {'dp'}, dimensions={0}, use_global_device_ids=true | all-gather | bytes 103680 | tf_op jit(solution)/shard_map/all_gather | solution.py:350
  169.8 0.6 multiply_bitcast_fusion
  170.4 0.0 copy-done.2
  170.4 0.0 copy-done.4
  170.4 0.0 copy-done.7
  170.4 3.3 %spatial_back.1 = (bf16[1728,128]{1,0:T(8,128)(2,1)}, bf16[128,1152]{1,0:T(8,128)(2,1)}) custom-call(bf16[8,24,1152]{2,1,0:T(8,128)(2,1)S(1)} %all_to_all.22.received, bf16[1152,576]{1,0:T(8,128)(2,1)S(1)} %copy-done.4, bf16[1728,128]{1,0:T(8,128)(2,1)S(1)} %bitcast.19, s32[1,1152]{1,0:T(1,128)S(1)} %copy-done.7), custom_call_target="tpu_custom_call" | custom-call | tf_op jit(solution)/shard_map/spatial_back/pallas_call | solution.py:263
  (1 shorter events, 0.0 us)
Async XLA Ops:
  0.6 1.0 copy-start.1
  1.6 1.0 copy-start.5
  4.8 35.3 %all-to-all-start = ((bf16[128,16,128]{2,1,0:T(8,128)(2,1)}), bf16[128,16,128]{2,1,0:T(8,128)(2,1)S(1)}, u32[]{:S(2)}, u32[]{:S(2)}) async-start(bf16[128,16,128]{2,1,0:T(8,128)(2,1)} %spatial_context.1), calls=%async_computation | async-start | bytes 1048576 | tf_op jit(solution)/shard_map/all_to_all | solution.py:281
  40.5 43.0 %copy-start.8 = (bf16[1,128,1,576]{1,3,2,0:T(8,128)(2,1)S(1)}, bf16[1,128,1,576]{1,3,2,0:T(8,128)(2,1)}, u32[]{:S(2)}) copy-start(bf16[1,128,1,576]{1,3,2,0:T(8,128)(2,1)} %param.9) | copy-start | bytes 442372
  40.5 43.1 %copy-start.6 = (s32[1,1152]{1,0:T(1,128)S(1)}, s32[1,1152]{1,0:T(1,128)}, u32[]{:S(2)}) copy-start(s32[1,1152]{1,0:T(1,128)} %constant.28.clone.feature_at) | copy-start | bytes 13828
  81.6 7.0 %copy-start = (bf16[16,72,1152]{2,1,0:T(8,128)(2,1)}, bf16[16,72,1152]{2,1,0:T(8,128)(2,1)S(1)}, u32[]{:S(2)}) copy-start(bf16[16,72,1152]{2,1,0:T(8,128)(2,1)S(1)} %all_to_all.20) | copy-start | bytes 7962628
  81.6 7.0 %collective-permute-start = (bf16[1152,1152]{1,0:T(8,128)(2,1)S(1)}, bf16[1152,1152]{1,0:T(8,128)(2,1)}, u32[]{:S(2)}, u32[]{:S(2)}) collective-permute-start(bf16[1152,1152]{1,0:T(8,128)(2,1)S(1)} %bitcast.15), channel_id=1, source_target_pairs={{0,64},{64,0},{128,192},{192,128},{256,320},{320,256},{384,448},{4... | collective-permute-start | bytes 7962632 | tf_op jit(solution)/shard_map/ppermute | solution.py:317
  97.2 1.1 copy-start.3
  126.9 43.5 %copy-start.2 = (bf16[1,1,128,1728]{2,3,1,0:T(8,128)(2,1)S(1)}, bf16[1,1,128,1728]{2,3,1,0:T(8,128)(2,1)}, u32[]{:S(2)}) copy-start(bf16[1,1,128,1728]{2,3,1,0:T(8,128)(2,1)} %param.8) | copy-start | bytes 1327108
  126.9 43.5 %copy-start.4 = (bf16[1152,576]{1,0:T(8,128)(2,1)S(1)}, bf16[1152,576]{1,0:T(8,128)(2,1)}, u32[]{:S(2)}) copy-start(bf16[1152,576]{1,0:T(8,128)(2,1)} %copy-done.3) | copy-start | bytes 3981316
  126.9 43.5 %copy-start.7 = (s32[1,1152]{1,0:T(1,128)S(1)}, s32[1,1152]{1,0:T(1,128)}, u32[]{:S(2)}) copy-start(s32[1,1152]{1,0:T(1,128)} %constant.29.clone.place_of) | copy-start | bytes 13828

commit v5 on v3

--- a/solution.py
+++ b/solution.py
@@ -139,9 +139,16 @@
     return jnp.concatenate([held[:, t, :] for t in range(first, first + count)], axis=1)
 
 
-def context_kernel(triple, hidden_there, tokens, held, hidden_in, arrived):
+def context_kernel(
+    triple, hidden_there, weight, out_t, tokens, packed, held, hidden_in, arrived
+):
     fetch = pltpu.make_async_copy(hidden_there, hidden_in, arrived)
     fetch.start()
+    w = weight[...].astype(F32)
+    o = out_t[...].astype(F32)
+    packed[0] = jnp.concatenate(
+        [w[:, :PART], o[:, :REST], w[:, PART:], o[:, REST:]], axis=1
+    ).astype(BF)
     context = attend_turned(
         triple[:INNER, :], triple[INNER:2 * INNER, :], triple[2 * INNER:, :]
     )
@@ -294,24 +301,21 @@
     cotangent = context_grad.reshape(TOKENS, INNER)
 
     core = (lax.axis_index("fx") % 2).astype(jnp.int32)[None]
-    out_t = out_weight.T
-    packed = jnp.concatenate(
-        [triple_weight[:, :PART], out_t[:, :REST], triple_weight[:, PART:], out_t[:, REST:]],
-        axis=1,
-    )
-    packed = lax.all_gather(packed[None], "fx", axis=0, tiled=True)
     slabs = (TOKENS, 16, 128)
     held = pltpu.VMEM(slabs, F32)
-    tokens = call(
+    tokens, packed = call(
         context_kernel,
         "spatial_context",
-        (slabs, BF),
+        [(slabs, BF), ((1, ROWS, 2 * D), BF)],
         spatial,
         hidden_in,
+        triple_weight,
+        out_weight.T,
         scratch=[held, pltpu.VMEM((TOKENS, D), BF), pltpu.SemaphoreType.DMA],
         there=(1,),
     )
     tokens = exchange(tokens, ("fx", "fy"))
+    packed = lax.all_gather(packed, "fx", axis=0, tiled=True)
     packed, tokens = lax.optimization_barrier((packed, tokens))
     near = call(
         forward_kernel,

time: 174 us -> 175 us (level)
  blocking collectives: 133 us -> 135 us
    all_gather x1, blocking collectives: 20.6 us -> 22.5 us  [local(): packed = lax.all_gather(packed, 'fx', axis=0, tiled=True)]
    slice x2 -> x0, local copies, waits for them, and re-layouts: 1.76 us -> none  [the longest x1 0.9 us: local(): triple_weight[:, PART:]]
    unnamed x17 -> x21, local copies, waits for them, and re-layouts: 3.67 us -> 5.23 us
  transfers between devices with their start and end apart: 2 -> 2, of which waited for: 0 -> 0; matrix products, arithmetic and copies ran while one was open for 1% -> 0% of each run, Pallas kernels for 2% -> 2%
where the time goes in v5:
time: 175 us
  blocking collectives  135 us (77%)
  Pallas kernels  18.6 us (11%)
  starting transfers between devices  14.8 us (8%)
  local copies, waits for them, and re-layouts  5.23 us (3%)
    all_to_all x3, blocking collectives, exchange(): return lax.all_to_all(x, axis, 0, 0, tiled=True)  88 us
    all_gather x1, blocking collectives, local(): totals = lax.all_gather(total, 'dp', axis=0, tiled=True)  24.2 us
    all_gather x1, blocking collectives, local(): packed = lax.all_gather(packed, 'fx', axis=0, tiled=True)  22.5 us
    pallas_call x7, Pallas kernels, call(): pl.pallas_call(kernel, out_shape=shapes if many else shapes[0], in_specs=...  18.6 us
    all_to_all x1, starting transfers between devices, exchange(): return lax.all_to_all(x, axis, 0, 0, tiled=True)  12.9 us
    unnamed x21, local copies, waits for them, and re-layouts  5.23 us
  transfers between devices with their start and end apart: 2, of which 0 were waited for; matrix products, arithmetic and copies ran while one was open for 0% of the time, Pallas kernels for 2%

profile of v5, /device:TPU:2, one launch (start us, length us, event | category | flops | bytes accessed | tf_op | source)
XLA Modules:
  0.0 174.7 jit_solution(18177620555791933443)
XLA Ops:
  0.6 0.0 copy-start.1
  0.6 1.0 copy-done.1
  1.6 0.0 copy-start.3
  1.6 1.0 copy-done.3
  2.6 0.0 copy-start.4
  2.6 0.8 copy-done.4
  3.4 0.0 copy-start.5
  3.4 0.7 copy-done.5
  4.2 2.6 %spatial_context.1 = (bf16[128,16,128]{2,1,0:T(8,128)(2,1)}, bf16[1,9,2304]{2,1,0:T(8,128)(2,1)S(1)}) custom-call(bf16[1728,128]{1,0:T(8,128)(2,1)S(1)} %bitcast.14, bf16[128,1152]{1,0:T(8,128)(2,1)S(1)} %bitcast.17, bf16[9,1728]{1,0:T(8,128)(2,1)S(1)} %copy-done.4, bf16[9,576]{1,0:T(8,128)(2,1)S(1)} %bitcast.18), custom_call_target="tpu_custom_call" | custom-call | tf_op jit(solution)/shard_map/spatial_context/pallas_call | solution.py:274
  6.7 12.9 %all-to-all-start = ((bf16[128,16,128]{2,1,0:T(8,128)(2,1)}), bf16[128,16,128]{2,1,0:T(8,128)(2,1)S(1)}, u32[]{:S(2)}, u32[]{:S(2)}) async-start(bf16[128,16,128]{2,1,0:T(8,128)(2,1)} %get-tuple-element.14), calls=%async_computation | async-start | bytes 1048576 | tf_op jit(solution)/shard_map/all_to_all | solution.py:295
  19.6 22.5 %all_gather.6.packed = bf16[8,9,2304]{2,1,0:T(8,128)(2,1)S(1)} all-gather(bf16[1,9,2304]{2,1,0:T(8,128)(2,1)S(1)} %get-tuple-element.13), channel_id=1, replica_groups=mesh['fx'=8,'fy'=16,'dp'=4] {'fx'}, dimensions={0}, use_global_device_ids=true | all-gather | bytes 373248 | tf_op jit(solution)/shard_map/all_gather | solution.py:318
  42.1 0.0 all-to-all-done.tokens
  42.1 0.3 forward.1
  42.4 0.0 copy-start.9
  42.4 0.0 copy-start.6
  42.4 41.0 %all_to_all.20 = bf16[16,72,1152]{2,1,0:T(8,128)(2,1)S(1)} all-to-all(bf16[16,72,1152]{2,1,0:T(8,128)(2,1)S(1)} %forward.1), channel_id=1, replica_groups=mesh['fx'=8,'fy'=16,'dp'=4] {'fy'}, dimensions={0} | all-to-all | bytes 5308416 | tf_op jit(solution)/shard_map/all_to_all | solution.py:295
  83.5 0.0 copy-start.8
  83.5 1.9 %collective-permute-start = (bf16[1152,1152]{1,0:T(8,128)(2,1)S(1)}, bf16[1152,1152]{1,0:T(8,128)(2,1)}, u32[]{:S(2)}, u32[]{:S(2)}) collective-permute-start(bf16[1152,1152]{1,0:T(8,128)(2,1)S(1)} %bitcast.19), channel_id=1, source_target_pairs={{0,64},{64,0},{128,192},{192,128},{256,320},{320,256},{384,448},{4... | collective-permute-start | bytes 7962632 | tf_op jit(solution)/shard_map/ppermute | solution.py:329
  85.4 0.0 copy-done.9
  85.4 0.2 copy.11
  85.6 0.0 copy-done.8
  85.6 0.0 copy-done.6
  85.6 3.3 %hidden_near.1 = (f32[128,1152]{1,0:T(8,128)S(1)}, bf16[1152,1152]{1,0:T(8,128)(2,1)S(1)}) custom-call(s32[1]{0:T(128)} %bitcast.core, bf16[1152,1152]{1,0:T(8,128)(2,1)} %bitcast.20, bf16[128,16,128]{2,1,0:T(8,128)(2,1)S(1)} %all-to-all-done.tokens, s32[1,1152]{1,0:T(1,128)S(1)} %copy-done.6), custom_call_target="tpu_custom_call" | custom-call | tf_op jit(solution)/shard_map/hidden_near/pallas_call | solution.py:274
  88.9 0.0 copy-start
  88.9 1.5 copy-done
  90.4 0.0 collective-permute-done.far
  90.4 8.6 %temporal_back.1 = (bf16[16,88,576]{2,1,0:T(8,128)(2,1)S(1)}, bf16[1152,576]{1,0:T(8,128)(2,1)S(1)}) custom-call(s32[1]{0:T(128)} %bitcast.core, bf16[1152,1152]{1,0:T(8,128)(2,1)} %copy-done, bf16[1152,1152]{1,0:T(8,128)(2,1)} %collective-permute-done.far, f32[128,1152]{1,0:T(8,128)S(1)} %get-tuple-element.18.placed, ...), custom_call_target="tpu_custom_call" | custom-call | tf_op jit(solution)/shard_map/temporal_back/pallas_call | solution.py:274
  99.1 29.0 %all_to_all.21.received = bf16[16,88,576]{2,1,0:T(8,128)(2,1)S(1)} all-to-all(bf16[16,88,576]{2,1,0:T(8,128)(2,1)S(1)} %get-tuple-element.19), channel_id=1, replica_groups=mesh['fx'=8,'fy'=16,'dp'=4] {'fy'}, dimensions={0} | all-to-all | bytes 3244032 | tf_op jit(solution)/shard_map/all_to_all | solution.py:295
  128.1 0.0 copy-start.2
  128.1 0.0 copy-start.7
  128.1 0.4 turn.1
  128.6 18.0 %all_to_all.22.received = bf16[8,24,1152]{2,1,0:T(8,128)(2,1)S(1)} all-to-all(bf16[8,24,1152]{2,1,0:T(8,128)(2,1)S(1)} %turn.1), channel_id=1, replica_groups=mesh['fx'=8,'fy'=16,'dp'=4] {'fx'}, dimensions={0} | all-to-all | bytes 884736 | tf_op jit(solution)/shard_map/all_to_all | solution.py:295
  146.5 0.1 weight_sum.1
  146.6 24.2 %all_gather.7 = f32[4,9,576]{2,1,0:T(8,128)S(1)} all-gather(f32[1,9,576]{2,1,0:T(8,128)S(1)} %weight_sum.1), channel_id=1, replica_groups=mesh['fx'=8,'fy'=16,'dp'=4] {'dp'}, dimensions={0}, use_global_device_ids=true | all-gather | bytes 103680 | tf_op jit(solution)/shard_map/all_gather | solution.py:362
  170.9 0.6 multiply_bitcast_fusion
  171.5 0.0 copy-done.2
  171.5 0.0 copy-done.7
  171.5 3.3 %spatial_back.1 = (bf16[1728,128]{1,0:T(8,128)(2,1)}, bf16[128,1152]{1,0:T(8,128)(2,1)}) custom-call(bf16[8,24,1152]{2,1,0:T(8,128)(2,1)S(1)} %all_to_all.22.received, bf16[1152,576]{1,0:T(8,128)(2,1)S(1)} %get-tuple-element.20.out_rows, bf16[1728,128]{1,0:T(8,128)(2,1)S(1)} %bitcast.15, s32[1,1152]{1,0:T(1,128)S(1)} %copy-done.7), custom_call_target="tpu_custom_call" | custom-call | tf_op jit(solution)/shard_map/spatial_back/pallas_call | solution.py:274
  (1 shorter events, 0.0 us)
Async XLA Ops:
  0.6 1.0 copy-start.1
  1.6 1.0 copy-start.3
  2.6 0.8 copy-start.4
  3.4 0.7 copy-start.5
  6.7 35.3 %all-to-all-start = ((bf16[128,16,128]{2,1,0:T(8,128)(2,1)}), bf16[128,16,128]{2,1,0:T(8,128)(2,1)S(1)}, u32[]{:S(2)}, u32[]{:S(2)}) async-start(bf16[128,16,128]{2,1,0:T(8,128)(2,1)} %get-tuple-element.14), calls=%async_computation | async-start | bytes 1048576 | tf_op jit(solution)/shard_map/all_to_all | solution.py:295
  42.4 43.0 %copy-start.9 = (bf16[1,128,1,576]{1,3,2,0:T(8,128)(2,1)S(1)}, bf16[1,128,1,576]{1,3,2,0:T(8,128)(2,1)}, u32[]{:S(2)}) copy-start(bf16[1,128,1,576]{1,3,2,0:T(8,128)(2,1)} %param.9) | copy-start | bytes 442372
  42.4 43.1 %copy-start.6 = (s32[1,1152]{1,0:T(1,128)S(1)}, s32[1,1152]{1,0:T(1,128)}, u32[]{:S(2)}) copy-start(s32[1,1152]{1,0:T(1,128)} %constant.28.clone.feature_at) | copy-start | bytes 13828
  83.5 2.1 %copy-start.8 = (bf16[16,72,1152]{2,1,0:T(8,128)(2,1)}, bf16[16,72,1152]{2,1,0:T(8,128)(2,1)S(1)}, u32[]{:S(2)}) copy-start(bf16[16,72,1152]{2,1,0:T(8,128)(2,1)S(1)} %all_to_all.20) | copy-start | bytes 7962628
  83.5 7.0 %collective-permute-start = (bf16[1152,1152]{1,0:T(8,128)(2,1)S(1)}, bf16[1152,1152]{1,0:T(8,128)(2,1)}, u32[]{:S(2)}, u32[]{:S(2)}) collective-permute-start(bf16[1152,1152]{1,0:T(8,128)(2,1)S(1)} %bitcast.19), channel_id=1, source_target_pairs={{0,64},{64,0},{128,192},{192,128},{256,320},{320,256},{384,448},{4... | collective-permute-start | bytes 7962632 | tf_op jit(solution)/shard_map/ppermute | solution.py:329
  88.9 1.5 copy-start
  128.1 43.4 %copy-start.2 = (bf16[1,1,128,1728]{2,3,1,0:T(8,128)(2,1)S(1)}, bf16[1,1,128,1728]{2,3,1,0:T(8,128)(2,1)}, u32[]{:S(2)}) copy-start(bf16[1,1,128,1728]{2,3,1,0:T(8,128)(2,1)} %param.8) | copy-start | bytes 1327108
  128.1 43.4 %copy-start.7 = (s32[1,1152]{1,0:T(1,128)S(1)}, s32[1,1152]{1,0:T(1,128)}, u32[]{:S(2)}) copy-start(s32[1,1152]{1,0:T(1,128)} %constant.29.clone.place_of) | copy-start | bytes 13828
